TPU v7x, 128 devices: a whole 4x4x4 slice. The times are simulated.
128 devices in a mesh: blk: 64 (over y, z_hi, x, core), rep: 2 (over z_lo).
Axes of the slice: x: 4, y: 4, z: 4 (z_hi: 2, z_lo: 2; z = z_hi * 2 + z_lo), core: 2. Of those that a mesh axis runs over, the one named last changes fastest.
Arguments:
- feature_codes: bfloat16 [32768, 512], P('blk', 'rep'), may hold values from -6 to 6
- group_scales: float32 [32768, 4], P('blk', 'rep'), may hold values from 0.25 to 2
- adjacency: bfloat16 [32768, 128, 128], P('blk'), may hold values from 0 to 2, as said below
- tile_source: int32 [32768], P('blk'), may hold values from 0 to 255, as said below
- tile_target: int32 [32768], P('blk'), may hold values from 0 to 3
- weight: bfloat16 [1024, 512], replicated, may hold values from -0.1875 to 0.1875
- out_bias: float32 [512], P('rep'), may hold values from -3 to 3
Outputs:
- hidden: bfloat16 [32768, 512], P('blk', 'rep')
Inputs may be any that keep to these rules, and one draw needn't show every extreme that they name: Entries 512 b to 512 (b + 1) - 1 are block b's tiles, in ascending order of tile_source; no two tiles of one block share both source and target tile. `adjacency`: entries are 0 or positive.
All inputs are finite; a program needn't handle non-finite values.
Results may differ from a plain program's by a relative error of at most 0.0052.
Values may be sent and summed in bfloat16 or wider, within the bound.
No kernel may reach another device: no remote copies, remote signals or barrier semaphores. Data moves between devices by JAX's collectives and lax.ppermute only.
A program may use at most 128 MiB of HBM per device.

v0:
```python
import jax
import jax.numpy as jnp
from jax import lax
from jax.sharding import PartitionSpec as P

F = 512
TILE = 128


def passed_along(value, axis, steps):
    count = lax.axis_size(axis)
    pairs = [(source, (source + steps) % count) for source in range(count)]
    return lax.ppermute(value, axis, pairs)


def body(feature_codes, group_scales, adjacency, tile_source, tile_target, weight, out_bias):
    rows, half = feature_codes.shape
    groups = group_scales.shape[1]
    scaled = (
        feature_codes.astype(jnp.float32).reshape(rows, groups, half // groups)
        * group_scales[:, :, None]
    )
    features = scaled.reshape(rows, half).astype(jnp.bfloat16)
    tiles_here = rows // TILE
    blocks_total = lax.axis_size("blk")
    block_self = lax.axis_index("blk")
    tile_count = adjacency.shape[0]

    def place(buffer, visitor, block_id):
        return lax.dynamic_update_slice_in_dim(buffer, visitor, block_id * rows, 0)

    empty = jnp.zeros((blocks_total * rows, half), jnp.bfloat16)

    def advance(section, carry):
        visitor, buffer = carry
        visitor = passed_along(visitor, "blk", 1)
        return (visitor, place(buffer, visitor, (block_self - section) % blocks_total))

    visitor, every_row = lax.fori_loop(
        1, blocks_total, advance, (features, place(empty, features, block_self))
    )
    node_tiles = every_row.reshape(-1, TILE, half)
    step = 32
    batches = tile_count // step
    tile_ids = jnp.arange(tiles_here, dtype=jnp.int32)

    def absorb(carry, inputs):
        running, degree = carry
        matrices, sources, targets = inputs
        picked = jnp.take(node_tiles, sources, axis=0)
        products = jnp.einsum("kij,kjf->kif", matrices, picked, preferred_element_type=jnp.float32)
        selector = (targets[:, None] == tile_ids[None, :]).astype(jnp.float32)
        running = running + jnp.einsum(
            "kn,kif->nif", selector, products, precision=lax.Precision.HIGHEST
        )
        row_sums = jnp.sum(matrices, axis=2, dtype=jnp.float32)
        degree = degree + jnp.einsum(
            "kn,ki->ni", selector, row_sums, precision=lax.Precision.HIGHEST
        )
        return ((running, degree), None)

    start_state = (
        jnp.zeros((tiles_here, TILE, half), jnp.float32),
        jnp.zeros((tiles_here, TILE), jnp.float32),
    )
    (totals, degree), unused = lax.scan(
        absorb,
        start_state,
        (
            adjacency.reshape(batches, step, TILE, TILE),
            tile_source.reshape(batches, step),
            tile_target.reshape(batches, step),
        ),
    )
    totals = totals.reshape(rows, half)
    neighbours = (totals / jnp.sqrt(1.0 + degree.reshape(rows, 1))).astype(jnp.bfloat16)
    slice_index = lax.axis_index("rep")
    out_cols = out_bias.shape[0]
    running = jnp.zeros((rows, out_cols), jnp.float32)
    start = jnp.int32(0)
    piece_self = lax.all_gather(features, "rep", axis=1, tiled=True)
    piece_near = lax.all_gather(neighbours, "rep", axis=1, tiled=True)
    count = piece_self.shape[1]
    column = slice_index * out_cols
    w_self = lax.dynamic_slice(weight, (start, column), (count, out_cols))
    w_near = lax.dynamic_slice(weight, (F + start, column), (count, out_cols))
    running = jnp.dot(piece_self, w_self, preferred_element_type=jnp.float32)
    summed = running + jnp.dot(piece_near, w_near, preferred_element_type=jnp.float32)
    return jnp.maximum(summed + out_bias, 0.0).astype(jnp.bfloat16)


def solution(mesh):
    placed = (
        P("blk", "rep"),
        P("blk", "rep"),
        P("blk", None, None),
        P("blk"),
        P("blk"),
        P(),
        P("rep"),
    )
    return jax.shard_map(
        body, mesh=mesh, in_specs=placed, out_specs=P("blk", "rep"), check_vma=False
    )
```

profile of v0, /device:TPU:1, one launch (start us, length us, event | category | flops | bytes accessed | tf_op | source)
XLA Modules:
  0.0 1089.8 jit_solution(2091909130774487607)
XLA Ops:
  8.2 764.8 %while.30 = (s32[]{:T(128)}, bf16[512,256]{1,0:T(8,128)(2,1)S(1)}, bf16[32768,256]{1,0:T(8,128)(2,1)}, s32[]{:T(128)}, s32[]{:T(128)}, /*index=5*/s32[]{:T(128)}, s32[]{:T(128)}, s32[]{:T(128)}, s32[]{:T(128)}, s32[]{:T(128)}) while((s32[]{:T(128)}, bf16[512,256]{1,0:T(8,128)(2,1)S(1)}, bf16[32768,256]{1,0:T(8,128)(2,1)}, s32[]{:T(128)}, ...), condition=%wide.region_1.2_spmd, body=%wide.region_0.1_spmd.sunk | while | flops 18 | bytes 2097464 | solution.py:39
  24.4 11.5 %collective-permute-done = bf16[512,256]{1,0:T(8,128)(2,1)S(1)} collective-permute-done((bf16[512,256]{1,0:T(8,128)(2,1)S(1)}, bf16[512,256]{1,0:T(8,128)(2,1)S(1)}, u32[]{:S(2)}, u32[]{:S(2)}) %collective-permute-start) | collective-permute-done | bytes 262176 | tf_op jit(solution)/shard_map/while/body/eval_jaxpr/ppermute | solution.py:13
  36.7 11.5 %collective-permute-done = bf16[512,256]{1,0:T(8,128)(2,1)S(1)} collective-permute-done((bf16[512,256]{1,0:T(8,128)(2,1)S(1)}, bf16[512,256]{1,0:T(8,128)(2,1)S(1)}, u32[]{:S(2)}, u32[]{:S(2)}) %collective-permute-start) | collective-permute-done | bytes 262176 | tf_op jit(solution)/shard_map/while/body/eval_jaxpr/ppermute | solution.py:13
  48.9 11.5 %collective-permute-done = bf16[512,256]{1,0:T(8,128)(2,1)S(1)} collective-permute-done((bf16[512,256]{1,0:T(8,128)(2,1)S(1)}, bf16[512,256]{1,0:T(8,128)(2,1)S(1)}, u32[]{:S(2)}, u32[]{:S(2)}) %collective-permute-start) | collective-permute-done | bytes 262176 | tf_op jit(solution)/shard_map/while/body/eval_jaxpr/ppermute | solution.py:13
  61.2 11.5 %collective-permute-done = bf16[512,256]{1,0:T(8,128)(2,1)S(1)} collective-permute-done((bf16[512,256]{1,0:T(8,128)(2,1)S(1)}, bf16[512,256]{1,0:T(8,128)(2,1)S(1)}, u32[]{:S(2)}, u32[]{:S(2)}) %collective-permute-start) | collective-permute-done | bytes 262176 | tf_op jit(solution)/shard_map/while/body/eval_jaxpr/ppermute | solution.py:13
  73.5 11.5 %collective-permute-done = bf16[512,256]{1,0:T(8,128)(2,1)S(1)} collective-permute-done((bf16[512,256]{1,0:T(8,128)(2,1)S(1)}, bf16[512,256]{1,0:T(8,128)(2,1)S(1)}, u32[]{:S(2)}, u32[]{:S(2)}) %collective-permute-start) | collective-permute-done | bytes 262176 | tf_op jit(solution)/shard_map/while/body/eval_jaxpr/ppermute | solution.py:13
  85.8 11.5 %collective-permute-done = bf16[512,256]{1,0:T(8,128)(2,1)S(1)} collective-permute-done((bf16[512,256]{1,0:T(8,128)(2,1)S(1)}, bf16[512,256]{1,0:T(8,128)(2,1)S(1)}, u32[]{:S(2)}, u32[]{:S(2)}) %collective-permute-start) | collective-permute-done | bytes 262176 | tf_op jit(solution)/shard_map/while/body/eval_jaxpr/ppermute | solution.py:13
  98.0 11.5 %collective-permute-done = bf16[512,256]{1,0:T(8,128)(2,1)S(1)} collective-permute-done((bf16[512,256]{1,0:T(8,128)(2,1)S(1)}, bf16[512,256]{1,0:T(8,128)(2,1)S(1)}, u32[]{:S(2)}, u32[]{:S(2)}) %collective-permute-start) | collective-permute-done | bytes 262176 | tf_op jit(solution)/shard_map/while/body/eval_jaxpr/ppermute | solution.py:13
  110.3 11.5 %collective-permute-done = bf16[512,256]{1,0:T(8,128)(2,1)S(1)} collective-permute-done((bf16[512,256]{1,0:T(8,128)(2,1)S(1)}, bf16[512,256]{1,0:T(8,128)(2,1)S(1)}, u32[]{:S(2)}, u32[]{:S(2)}) %collective-permute-start) | collective-permute-done | bytes 262176 | tf_op jit(solution)/shard_map/while/body/eval_jaxpr/ppermute | solution.py:13
  122.5 11.5 %collective-permute-done = bf16[512,256]{1,0:T(8,128)(2,1)S(1)} collective-permute-done((bf16[512,256]{1,0:T(8,128)(2,1)S(1)}, bf16[512,256]{1,0:T(8,128)(2,1)S(1)}, u32[]{:S(2)}, u32[]{:S(2)}) %collective-permute-start) | collective-permute-done | bytes 262176 | tf_op jit(solution)/shard_map/while/body/eval_jaxpr/ppermute | solution.py:13
  134.8 11.5 %collective-permute-done = bf16[512,256]{1,0:T(8,128)(2,1)S(1)} collective-permute-done((bf16[512,256]{1,0:T(8,128)(2,1)S(1)}, bf16[512,256]{1,0:T(8,128)(2,1)S(1)}, u32[]{:S(2)}, u32[]{:S(2)}) %collective-permute-start) | collective-permute-done | bytes 262176 | tf_op jit(solution)/shard_map/while/body/eval_jaxpr/ppermute | solution.py:13
  147.1 11.5 %collective-permute-done = bf16[512,256]{1,0:T(8,128)(2,1)S(1)} collective-permute-done((bf16[512,256]{1,0:T(8,128)(2,1)S(1)}, bf16[512,256]{1,0:T(8,128)(2,1)S(1)}, u32[]{:S(2)}, u32[]{:S(2)}) %collective-permute-start) | collective-permute-done | bytes 262176 | tf_op jit(solution)/shard_map/while/body/eval_jaxpr/ppermute | solution.py:13
  159.3 11.5 %collective-permute-done = bf16[512,256]{1,0:T(8,128)(2,1)S(1)} collective-permute-done((bf16[512,256]{1,0:T(8,128)(2,1)S(1)}, bf16[512,256]{1,0:T(8,128)(2,1)S(1)}, u32[]{:S(2)}, u32[]{:S(2)}) %collective-permute-start) | collective-permute-done | bytes 262176 | tf_op jit(solution)/shard_map/while/body/eval_jaxpr/ppermute | solution.py:13
  171.6 11.5 %collective-permute-done = bf16[512,256]{1,0:T(8,128)(2,1)S(1)} collective-permute-done((bf16[512,256]{1,0:T(8,128)(2,1)S(1)}, bf16[512,256]{1,0:T(8,128)(2,1)S(1)}, u32[]{:S(2)}, u32[]{:S(2)}) %collective-permute-start) | collective-permute-done | bytes 262176 | tf_op jit(solution)/shard_map/while/body/eval_jaxpr/ppermute | solution.py:13
  183.9 11.5 %collective-permute-done = bf16[512,256]{1,0:T(8,128)(2,1)S(1)} collective-permute-done((bf16[512,256]{1,0:T(8,128)(2,1)S(1)}, bf16[512,256]{1,0:T(8,128)(2,1)S(1)}, u32[]{:S(2)}, u32[]{:S(2)}) %collective-permute-start) | collective-permute-done | bytes 262176 | tf_op jit(solution)/shard_map/while/body/eval_jaxpr/ppermute | solution.py:13
  196.2 11.5 %collective-permute-done = bf16[512,256]{1,0:T(8,128)(2,1)S(1)} collective-permute-done((bf16[512,256]{1,0:T(8,128)(2,1)S(1)}, bf16[512,256]{1,0:T(8,128)(2,1)S(1)}, u32[]{:S(2)}, u32[]{:S(2)}) %collective-permute-start) | collective-permute-done | bytes 262176 | tf_op jit(solution)/shard_map/while/body/eval_jaxpr/ppermute | solution.py:13
  208.5 11.5 %collective-permute-done = bf16[512,256]{1,0:T(8,128)(2,1)S(1)} collective-permute-done((bf16[512,256]{1,0:T(8,128)(2,1)S(1)}, bf16[512,256]{1,0:T(8,128)(2,1)S(1)}, u32[]{:S(2)}, u32[]{:S(2)}) %collective-permute-start) | collective-permute-done | bytes 262176 | tf_op jit(solution)/shard_map/while/body/eval_jaxpr/ppermute | solution.py:13
  220.8 11.5 %collective-permute-done = bf16[512,256]{1,0:T(8,128)(2,1)S(1)} collective-permute-done((bf16[512,256]{1,0:T(8,128)(2,1)S(1)}, bf16[512,256]{1,0:T(8,128)(2,1)S(1)}, u32[]{:S(2)}, u32[]{:S(2)}) %collective-permute-start) | collective-permute-done | bytes 262176 | tf_op jit(solution)/shard_map/while/body/eval_jaxpr/ppermute | solution.py:13
  233.0 11.5 %collective-permute-done = bf16[512,256]{1,0:T(8,128)(2,1)S(1)} collective-permute-done((bf16[512,256]{1,0:T(8,128)(2,1)S(1)}, bf16[512,256]{1,0:T(8,128)(2,1)S(1)}, u32[]{:S(2)}, u32[]{:S(2)}) %collective-permute-start) | collective-permute-done | bytes 262176 | tf_op jit(solution)/shard_map/while/body/eval_jaxpr/ppermute | solution.py:13
  245.3 11.5 %collective-permute-done = bf16[512,256]{1,0:T(8,128)(2,1)S(1)} collective-permute-done((bf16[512,256]{1,0:T(8,128)(2,1)S(1)}, bf16[512,256]{1,0:T(8,128)(2,1)S(1)}, u32[]{:S(2)}, u32[]{:S(2)}) %collective-permute-start) | collective-permute-done | bytes 262176 | tf_op jit(solution)/shard_map/while/body/eval_jaxpr/ppermute | solution.py:13
  257.6 11.5 %collective-permute-done = bf16[512,256]{1,0:T(8,128)(2,1)S(1)} collective-permute-done((bf16[512,256]{1,0:T(8,128)(2,1)S(1)}, bf16[512,256]{1,0:T(8,128)(2,1)S(1)}, u32[]{:S(2)}, u32[]{:S(2)}) %collective-permute-start) | collective-permute-done | bytes 262176 | tf_op jit(solution)/shard_map/while/body/eval_jaxpr/ppermute | solution.py:13
  269.8 11.5 %collective-permute-done = bf16[512,256]{1,0:T(8,128)(2,1)S(1)} collective-permute-done((bf16[512,256]{1,0:T(8,128)(2,1)S(1)}, bf16[512,256]{1,0:T(8,128)(2,1)S(1)}, u32[]{:S(2)}, u32[]{:S(2)}) %collective-permute-start) | collective-permute-done | bytes 262176 | tf_op jit(solution)/shard_map/while/body/eval_jaxpr/ppermute | solution.py:13
  282.1 11.5 %collective-permute-done = bf16[512,256]{1,0:T(8,128)(2,1)S(1)} collective-permute-done((bf16[512,256]{1,0:T(8,128)(2,1)S(1)}, bf16[512,256]{1,0:T(8,128)(2,1)S(1)}, u32[]{:S(2)}, u32[]{:S(2)}) %collective-permute-start) | collective-permute-done | bytes 262176 | tf_op jit(solution)/shard_map/while/body/eval_jaxpr/ppermute | solution.py:13
  294.4 11.5 %collective-permute-done = bf16[512,256]{1,0:T(8,128)(2,1)S(1)} collective-permute-done((bf16[512,256]{1,0:T(8,128)(2,1)S(1)}, bf16[512,256]{1,0:T(8,128)(2,1)S(1)}, u32[]{:S(2)}, u32[]{:S(2)}) %collective-permute-start) | collective-permute-done | bytes 262176 | tf_op jit(solution)/shard_map/while/body/eval_jaxpr/ppermute | solution.py:13
  306.6 11.5 %collective-permute-done = bf16[512,256]{1,0:T(8,128)(2,1)S(1)} collective-permute-done((bf16[512,256]{1,0:T(8,128)(2,1)S(1)}, bf16[512,256]{1,0:T(8,128)(2,1)S(1)}, u32[]{:S(2)}, u32[]{:S(2)}) %collective-permute-start) | collective-permute-done | bytes 262176 | tf_op jit(solution)/shard_map/while/body/eval_jaxpr/ppermute | solution.py:13
  318.9 11.5 %collective-permute-done = bf16[512,256]{1,0:T(8,128)(2,1)S(1)} collective-permute-done((bf16[512,256]{1,0:T(8,128)(2,1)S(1)}, bf16[512,256]{1,0:T(8,128)(2,1)S(1)}, u32[]{:S(2)}, u32[]{:S(2)}) %collective-permute-start) | collective-permute-done | bytes 262176 | tf_op jit(solution)/shard_map/while/body/eval_jaxpr/ppermute | solution.py:13
  331.2 11.5 %collective-permute-done = bf16[512,256]{1,0:T(8,128)(2,1)S(1)} collective-permute-done((bf16[512,256]{1,0:T(8,128)(2,1)S(1)}, bf16[512,256]{1,0:T(8,128)(2,1)S(1)}, u32[]{:S(2)}, u32[]{:S(2)}) %collective-permute-start) | collective-permute-done | bytes 262176 | tf_op jit(solution)/shard_map/while/body/eval_jaxpr/ppermute | solution.py:13
  343.4 11.5 %collective-permute-done = bf16[512,256]{1,0:T(8,128)(2,1)S(1)} collective-permute-done((bf16[512,256]{1,0:T(8,128)(2,1)S(1)}, bf16[512,256]{1,0:T(8,128)(2,1)S(1)}, u32[]{:S(2)}, u32[]{:S(2)}) %collective-permute-start) | collective-permute-done | bytes 262176 | tf_op jit(solution)/shard_map/while/body/eval_jaxpr/ppermute | solution.py:13
  355.7 11.6 %collective-permute-done = bf16[512,256]{1,0:T(8,128)(2,1)S(1)} collective-permute-done((bf16[512,256]{1,0:T(8,128)(2,1)S(1)}, bf16[512,256]{1,0:T(8,128)(2,1)S(1)}, u32[]{:S(2)}, u32[]{:S(2)}) %collective-permute-start) | collective-permute-done | bytes 262176 | tf_op jit(solution)/shard_map/while/body/eval_jaxpr/ppermute | solution.py:13
  368.0 11.5 %collective-permute-done = bf16[512,256]{1,0:T(8,128)(2,1)S(1)} collective-permute-done((bf16[512,256]{1,0:T(8,128)(2,1)S(1)}, bf16[512,256]{1,0:T(8,128)(2,1)S(1)}, u32[]{:S(2)}, u32[]{:S(2)}) %collective-permute-start) | collective-permute-done | bytes 262176 | tf_op jit(solution)/shard_map/while/body/eval_jaxpr/ppermute | solution.py:13
  380.3 11.5 %collective-permute-done = bf16[512,256]{1,0:T(8,128)(2,1)S(1)} collective-permute-done((bf16[512,256]{1,0:T(8,128)(2,1)S(1)}, bf16[512,256]{1,0:T(8,128)(2,1)S(1)}, u32[]{:S(2)}, u32[]{:S(2)}) %collective-permute-start) | collective-permute-done | bytes 262176 | tf_op jit(solution)/shard_map/while/body/eval_jaxpr/ppermute | solution.py:13
  392.6 11.5 %collective-permute-done = bf16[512,256]{1,0:T(8,128)(2,1)S(1)} collective-permute-done((bf16[512,256]{1,0:T(8,128)(2,1)S(1)}, bf16[512,256]{1,0:T(8,128)(2,1)S(1)}, u32[]{:S(2)}, u32[]{:S(2)}) %collective-permute-start) | collective-permute-done | bytes 262176 | tf_op jit(solution)/shard_map/while/body/eval_jaxpr/ppermute | solution.py:13
  404.9 11.5 %collective-permute-done = bf16[512,256]{1,0:T(8,128)(2,1)S(1)} collective-permute-done((bf16[512,256]{1,0:T(8,128)(2,1)S(1)}, bf16[512,256]{1,0:T(8,128)(2,1)S(1)}, u32[]{:S(2)}, u32[]{:S(2)}) %collective-permute-start) | collective-permute-done | bytes 262176 | tf_op jit(solution)/shard_map/while/body/eval_jaxpr/ppermute | solution.py:13
  417.2 11.5 %collective-permute-done = bf16[512,256]{1,0:T(8,128)(2,1)S(1)} collective-permute-done((bf16[512,256]{1,0:T(8,128)(2,1)S(1)}, bf16[512,256]{1,0:T(8,128)(2,1)S(1)}, u32[]{:S(2)}, u32[]{:S(2)}) %collective-permute-start) | collective-permute-done | bytes 262176 | tf_op jit(solution)/shard_map/while/body/eval_jaxpr/ppermute | solution.py:13
  429.4 11.5 %collective-permute-done = bf16[512,256]{1,0:T(8,128)(2,1)S(1)} collective-permute-done((bf16[512,256]{1,0:T(8,128)(2,1)S(1)}, bf16[512,256]{1,0:T(8,128)(2,1)S(1)}, u32[]{:S(2)}, u32[]{:S(2)}) %collective-permute-start) | collective-permute-done | bytes 262176 | tf_op jit(solution)/shard_map/while/body/eval_jaxpr/ppermute | solution.py:13
  441.7 11.5 %collective-permute-done = bf16[512,256]{1,0:T(8,128)(2,1)S(1)} collective-permute-done((bf16[512,256]{1,0:T(8,128)(2,1)S(1)}, bf16[512,256]{1,0:T(8,128)(2,1)S(1)}, u32[]{:S(2)}, u32[]{:S(2)}) %collective-permute-start) | collective-permute-done | bytes 262176 | tf_op jit(solution)/shard_map/while/body/eval_jaxpr/ppermute | solution.py:13
  454.0 11.5 %collective-permute-done = bf16[512,256]{1,0:T(8,128)(2,1)S(1)} collective-permute-done((bf16[512,256]{1,0:T(8,128)(2,1)S(1)}, bf16[512,256]{1,0:T(8,128)(2,1)S(1)}, u32[]{:S(2)}, u32[]{:S(2)}) %collective-permute-start) | collective-permute-done | bytes 262176 | tf_op jit(solution)/shard_map/while/body/eval_jaxpr/ppermute | solution.py:13
  466.3 11.5 %collective-permute-done = bf16[512,256]{1,0:T(8,128)(2,1)S(1)} collective-permute-done((bf16[512,256]{1,0:T(8,128)(2,1)S(1)}, bf16[512,256]{1,0:T(8,128)(2,1)S(1)}, u32[]{:S(2)}, u32[]{:S(2)}) %collective-permute-start) | collective-permute-done | bytes 262176 | tf_op jit(solution)/shard_map/while/body/eval_jaxpr/ppermute | solution.py:13
  478.5 11.5 %collective-permute-done = bf16[512,256]{1,0:T(8,128)(2,1)S(1)} collective-permute-done((bf16[512,256]{1,0:T(8,128)(2,1)S(1)}, bf16[512,256]{1,0:T(8,128)(2,1)S(1)}, u32[]{:S(2)}, u32[]{:S(2)}) %collective-permute-start) | collective-permute-done | bytes 262176 | tf_op jit(solution)/shard_map/while/body/eval_jaxpr/ppermute | solution.py:13
  490.8 11.5 %collective-permute-done = bf16[512,256]{1,0:T(8,128)(2,1)S(1)} collective-permute-done((bf16[512,256]{1,0:T(8,128)(2,1)S(1)}, bf16[512,256]{1,0:T(8,128)(2,1)S(1)}, u32[]{:S(2)}, u32[]{:S(2)}) %collective-permute-start) | collective-permute-done | bytes 262176 | tf_op jit(solution)/shard_map/while/body/eval_jaxpr/ppermute | solution.py:13
  503.0 11.5 %collective-permute-done = bf16[512,256]{1,0:T(8,128)(2,1)S(1)} collective-permute-done((bf16[512,256]{1,0:T(8,128)(2,1)S(1)}, bf16[512,256]{1,0:T(8,128)(2,1)S(1)}, u32[]{:S(2)}, u32[]{:S(2)}) %collective-permute-start) | collective-permute-done | bytes 262176 | tf_op jit(solution)/shard_map/while/body/eval_jaxpr/ppermute | solution.py:13
  515.3 11.5 %collective-permute-done = bf16[512,256]{1,0:T(8,128)(2,1)S(1)} collective-permute-done((bf16[512,256]{1,0:T(8,128)(2,1)S(1)}, bf16[512,256]{1,0:T(8,128)(2,1)S(1)}, u32[]{:S(2)}, u32[]{:S(2)}) %collective-permute-start) | collective-permute-done | bytes 262176 | tf_op jit(solution)/shard_map/while/body/eval_jaxpr/ppermute | solution.py:13
  527.6 11.5 %collective-permute-done = bf16[512,256]{1,0:T(8,128)(2,1)S(1)} collective-permute-done((bf16[512,256]{1,0:T(8,128)(2,1)S(1)}, bf16[512,256]{1,0:T(8,128)(2,1)S(1)}, u32[]{:S(2)}, u32[]{:S(2)}) %collective-permute-start) | collective-permute-done | bytes 262176 | tf_op jit(solution)/shard_map/while/body/eval_jaxpr/ppermute | solution.py:13
  539.9 11.5 %collective-permute-done = bf16[512,256]{1,0:T(8,128)(2,1)S(1)} collective-permute-done((bf16[512,256]{1,0:T(8,128)(2,1)S(1)}, bf16[512,256]{1,0:T(8,128)(2,1)S(1)}, u32[]{:S(2)}, u32[]{:S(2)}) %collective-permute-start) | collective-permute-done | bytes 262176 | tf_op jit(solution)/shard_map/while/body/eval_jaxpr/ppermute | solution.py:13
  552.1 11.5 %collective-permute-done = bf16[512,256]{1,0:T(8,128)(2,1)S(1)} collective-permute-done((bf16[512,256]{1,0:T(8,128)(2,1)S(1)}, bf16[512,256]{1,0:T(8,128)(2,1)S(1)}, u32[]{:S(2)}, u32[]{:S(2)}) %collective-permute-start) | collective-permute-done | bytes 262176 | tf_op jit(solution)/shard_map/while/body/eval_jaxpr/ppermute | solution.py:13
  564.4 11.5 %collective-permute-done = bf16[512,256]{1,0:T(8,128)(2,1)S(1)} collective-permute-done((bf16[512,256]{1,0:T(8,128)(2,1)S(1)}, bf16[512,256]{1,0:T(8,128)(2,1)S(1)}, u32[]{:S(2)}, u32[]{:S(2)}) %collective-permute-start) | collective-permute-done | bytes 262176 | tf_op jit(solution)/shard_map/while/body/eval_jaxpr/ppermute | solution.py:13
  576.7 11.5 %collective-permute-done = bf16[512,256]{1,0:T(8,128)(2,1)S(1)} collective-permute-done((bf16[512,256]{1,0:T(8,128)(2,1)S(1)}, bf16[512,256]{1,0:T(8,128)(2,1)S(1)}, u32[]{:S(2)}, u32[]{:S(2)}) %collective-permute-start) | collective-permute-done | bytes 262176 | tf_op jit(solution)/shard_map/while/body/eval_jaxpr/ppermute | solution.py:13
  589.0 11.5 %collective-permute-done = bf16[512,256]{1,0:T(8,128)(2,1)S(1)} collective-permute-done((bf16[512,256]{1,0:T(8,128)(2,1)S(1)}, bf16[512,256]{1,0:T(8,128)(2,1)S(1)}, u32[]{:S(2)}, u32[]{:S(2)}) %collective-permute-start) | collective-permute-done | bytes 262176 | tf_op jit(solution)/shard_map/while/body/eval_jaxpr/ppermute | solution.py:13
  601.3 11.5 %collective-permute-done = bf16[512,256]{1,0:T(8,128)(2,1)S(1)} collective-permute-done((bf16[512,256]{1,0:T(8,128)(2,1)S(1)}, bf16[512,256]{1,0:T(8,128)(2,1)S(1)}, u32[]{:S(2)}, u32[]{:S(2)}) %collective-permute-start) | collective-permute-done | bytes 262176 | tf_op jit(solution)/shard_map/while/body/eval_jaxpr/ppermute | solution.py:13
  613.5 11.5 %collective-permute-done = bf16[512,256]{1,0:T(8,128)(2,1)S(1)} collective-permute-done((bf16[512,256]{1,0:T(8,128)(2,1)S(1)}, bf16[512,256]{1,0:T(8,128)(2,1)S(1)}, u32[]{:S(2)}, u32[]{:S(2)}) %collective-permute-start) | collective-permute-done | bytes 262176 | tf_op jit(solution)/shard_map/while/body/eval_jaxpr/ppermute | solution.py:13
  625.8 11.5 %collective-permute-done = bf16[512,256]{1,0:T(8,128)(2,1)S(1)} collective-permute-done((bf16[512,256]{1,0:T(8,128)(2,1)S(1)}, bf16[512,256]{1,0:T(8,128)(2,1)S(1)}, u32[]{:S(2)}, u32[]{:S(2)}) %collective-permute-start) | collective-permute-done | bytes 262176 | tf_op jit(solution)/shard_map/while/body/eval_jaxpr/ppermute | solution.py:13
  638.0 11.5 %collective-permute-done = bf16[512,256]{1,0:T(8,128)(2,1)S(1)} collective-permute-done((bf16[512,256]{1,0:T(8,128)(2,1)S(1)}, bf16[512,256]{1,0:T(8,128)(2,1)S(1)}, u32[]{:S(2)}, u32[]{:S(2)}) %collective-permute-start) | collective-permute-done | bytes 262176 | tf_op jit(solution)/shard_map/while/body/eval_jaxpr/ppermute | solution.py:13
  650.3 11.5 %collective-permute-done = bf16[512,256]{1,0:T(8,128)(2,1)S(1)} collective-permute-done((bf16[512,256]{1,0:T(8,128)(2,1)S(1)}, bf16[512,256]{1,0:T(8,128)(2,1)S(1)}, u32[]{:S(2)}, u32[]{:S(2)}) %collective-permute-start) | collective-permute-done | bytes 262176 | tf_op jit(solution)/shard_map/while/body/eval_jaxpr/ppermute | solution.py:13
  662.6 11.5 %collective-permute-done = bf16[512,256]{1,0:T(8,128)(2,1)S(1)} collective-permute-done((bf16[512,256]{1,0:T(8,128)(2,1)S(1)}, bf16[512,256]{1,0:T(8,128)(2,1)S(1)}, u32[]{:S(2)}, u32[]{:S(2)}) %collective-permute-start) | collective-permute-done | bytes 262176 | tf_op jit(solution)/shard_map/while/body/eval_jaxpr/ppermute | solution.py:13
  674.9 11.5 %collective-permute-done = bf16[512,256]{1,0:T(8,128)(2,1)S(1)} collective-permute-done((bf16[512,256]{1,0:T(8,128)(2,1)S(1)}, bf16[512,256]{1,0:T(8,128)(2,1)S(1)}, u32[]{:S(2)}, u32[]{:S(2)}) %collective-permute-start) | collective-permute-done | bytes 262176 | tf_op jit(solution)/shard_map/while/body/eval_jaxpr/ppermute | solution.py:13
  687.2 11.5 %collective-permute-done = bf16[512,256]{1,0:T(8,128)(2,1)S(1)} collective-permute-done((bf16[512,256]{1,0:T(8,128)(2,1)S(1)}, bf16[512,256]{1,0:T(8,128)(2,1)S(1)}, u32[]{:S(2)}, u32[]{:S(2)}) %collective-permute-start) | collective-permute-done | bytes 262176 | tf_op jit(solution)/shard_map/while/body/eval_jaxpr/ppermute | solution.py:13
  699.4 11.5 %collective-permute-done = bf16[512,256]{1,0:T(8,128)(2,1)S(1)} collective-permute-done((bf16[512,256]{1,0:T(8,128)(2,1)S(1)}, bf16[512,256]{1,0:T(8,128)(2,1)S(1)}, u32[]{:S(2)}, u32[]{:S(2)}) %collective-permute-start) | collective-permute-done | bytes 262176 | tf_op jit(solution)/shard_map/while/body/eval_jaxpr/ppermute | solution.py:13
  711.7 11.5 %collective-permute-done = bf16[512,256]{1,0:T(8,128)(2,1)S(1)} collective-permute-done((bf16[512,256]{1,0:T(8,128)(2,1)S(1)}, bf16[512,256]{1,0:T(8,128)(2,1)S(1)}, u32[]{:S(2)}, u32[]{:S(2)}) %collective-permute-start) | collective-permute-done | bytes 262176 | tf_op jit(solution)/shard_map/while/body/eval_jaxpr/ppermute | solution.py:13
  723.9 11.5 %collective-permute-done = bf16[512,256]{1,0:T(8,128)(2,1)S(1)} collective-permute-done((bf16[512,256]{1,0:T(8,128)(2,1)S(1)}, bf16[512,256]{1,0:T(8,128)(2,1)S(1)}, u32[]{:S(2)}, u32[]{:S(2)}) %collective-permute-start) | collective-permute-done | bytes 262176 | tf_op jit(solution)/shard_map/while/body/eval_jaxpr/ppermute | solution.py:13
  736.2 11.5 %collective-permute-done = bf16[512,256]{1,0:T(8,128)(2,1)S(1)} collective-permute-done((bf16[512,256]{1,0:T(8,128)(2,1)S(1)}, bf16[512,256]{1,0:T(8,128)(2,1)S(1)}, u32[]{:S(2)}, u32[]{:S(2)}) %collective-permute-start) | collective-permute-done | bytes 262176 | tf_op jit(solution)/shard_map/while/body/eval_jaxpr/ppermute | solution.py:13
  748.5 11.5 %collective-permute-done = bf16[512,256]{1,0:T(8,128)(2,1)S(1)} collective-permute-done((bf16[512,256]{1,0:T(8,128)(2,1)S(1)}, bf16[512,256]{1,0:T(8,128)(2,1)S(1)}, u32[]{:S(2)}, u32[]{:S(2)}) %collective-permute-start) | collective-permute-done | bytes 262176 | tf_op jit(solution)/shard_map/while/body/eval_jaxpr/ppermute | solution.py:13
  760.7 11.5 %collective-permute-done = bf16[512,256]{1,0:T(8,128)(2,1)S(1)} collective-permute-done((bf16[512,256]{1,0:T(8,128)(2,1)S(1)}, bf16[512,256]{1,0:T(8,128)(2,1)S(1)}, u32[]{:S(2)}, u32[]{:S(2)}) %collective-permute-start) | collective-permute-done | bytes 262176 | tf_op jit(solution)/shard_map/while/body/eval_jaxpr/ppermute | solution.py:13
  773.2 302.2 %while.31 = (s32[]{:T(128)}, f32[4,128,256]{2,0,1:T(4,128)}, f32[4,128]{1,0:T(4,128)S(1)}, s32[16,32]{1,0:T(8,128)S(1)}, bf16[16,32,128,128]{3,2,1,0:T(8,128)(2,...) while((s32[]{:T(128)}, f32[4,128,256]{2,0,1:T(4,128)}, ...), condition=%wide.region_4.5_spmd.clone, body=%wide.region_2.4_spmd.clone.sunk | while | flops 321321504 | bytes 17868600 | solution.py:66
  821.3 6.7 fusion.52
  (360 shorter events, 379.6 us)
Async XLA Ops:
  0.0 1088.5 %copy-start = (bf16[1024,512]{1,0:T(8,128)(2,1)S(1)}, bf16[1024,512]{1,0:T(8,128)(2,1)}, u32[]{:S(2)}) copy-start(bf16[1024,512]{1,0:T(8,128)(2,1)} %param.16) | copy-start | bytes 3145732
  8.2 6.0 collective-permute-start
  15.0 8.7 collective-permute-start
  24.4 11.5 %collective-permute-start = (bf16[512,256]{1,0:T(8,128)(2,1)S(1)}, bf16[512,256]{1,0:T(8,128)(2,1)S(1)}, u32[]{:S(2)}, u32[]{:S(2)}) collective-permute-start(bf16[512,256]{1,0:T(8,128)(2,1)S(1)} %get-tuple-element.291), channel_id=1, source_target_pairs={{0,2},{2,4},{4,6},{6,8},{8,10},{10,12},{12,14},{14,16},{16,18},{18... | collective-permute-start | bytes 786440 | tf_op jit(solution)/shard_map/while/body/eval_jaxpr/ppermute | solution.py:13
  36.6 11.5 %collective-permute-start = (bf16[512,256]{1,0:T(8,128)(2,1)S(1)}, bf16[512,256]{1,0:T(8,128)(2,1)S(1)}, u32[]{:S(2)}, u32[]{:S(2)}) collective-permute-start(bf16[512,256]{1,0:T(8,128)(2,1)S(1)} %get-tuple-element.291), channel_id=1, source_target_pairs={{0,2},{2,4},{4,6},{6,8},{8,10},{10,12},{12,14},{14,16},{16,18},{18... | collective-permute-start | bytes 786440 | tf_op jit(solution)/shard_map/while/body/eval_jaxpr/ppermute | solution.py:13
  48.9 11.5 %collective-permute-start = (bf16[512,256]{1,0:T(8,128)(2,1)S(1)}, bf16[512,256]{1,0:T(8,128)(2,1)S(1)}, u32[]{:S(2)}, u32[]{:S(2)}) collective-permute-start(bf16[512,256]{1,0:T(8,128)(2,1)S(1)} %get-tuple-element.291), channel_id=1, source_target_pairs={{0,2},{2,4},{4,6},{6,8},{8,10},{10,12},{12,14},{14,16},{16,18},{18... | collective-permute-start | bytes 786440 | tf_op jit(solution)/shard_map/while/body/eval_jaxpr/ppermute | solution.py:13
  61.2 11.5 %collective-permute-start = (bf16[512,256]{1,0:T(8,128)(2,1)S(1)}, bf16[512,256]{1,0:T(8,128)(2,1)S(1)}, u32[]{:S(2)}, u32[]{:S(2)}) collective-permute-start(bf16[512,256]{1,0:T(8,128)(2,1)S(1)} %get-tuple-element.291), channel_id=1, source_target_pairs={{0,2},{2,4},{4,6},{6,8},{8,10},{10,12},{12,14},{14,16},{16,18},{18... | collective-permute-start | bytes 786440 | tf_op jit(solution)/shard_map/while/body/eval_jaxpr/ppermute | solution.py:13
  73.5 11.5 %collective-permute-start = (bf16[512,256]{1,0:T(8,128)(2,1)S(1)}, bf16[512,256]{1,0:T(8,128)(2,1)S(1)}, u32[]{:S(2)}, u32[]{:S(2)}) collective-permute-start(bf16[512,256]{1,0:T(8,128)(2,1)S(1)} %get-tuple-element.291), channel_id=1, source_target_pairs={{0,2},{2,4},{4,6},{6,8},{8,10},{10,12},{12,14},{14,16},{16,18},{18... | collective-permute-start | bytes 786440 | tf_op jit(solution)/shard_map/while/body/eval_jaxpr/ppermute | solution.py:13
  85.8 11.5 %collective-permute-start = (bf16[512,256]{1,0:T(8,128)(2,1)S(1)}, bf16[512,256]{1,0:T(8,128)(2,1)S(1)}, u32[]{:S(2)}, u32[]{:S(2)}) collective-permute-start(bf16[512,256]{1,0:T(8,128)(2,1)S(1)} %get-tuple-element.291), channel_id=1, source_target_pairs={{0,2},{2,4},{4,6},{6,8},{8,10},{10,12},{12,14},{14,16},{16,18},{18... | collective-permute-start | bytes 786440 | tf_op jit(solution)/shard_map/while/body/eval_jaxpr/ppermute | solution.py:13
  98.0 11.5 %collective-permute-start = (bf16[512,256]{1,0:T(8,128)(2,1)S(1)}, bf16[512,256]{1,0:T(8,128)(2,1)S(1)}, u32[]{:S(2)}, u32[]{:S(2)}) collective-permute-start(bf16[512,256]{1,0:T(8,128)(2,1)S(1)} %get-tuple-element.291), channel_id=1, source_target_pairs={{0,2},{2,4},{4,6},{6,8},{8,10},{10,12},{12,14},{14,16},{16,18},{18... | collective-permute-start | bytes 786440 | tf_op jit(solution)/shard_map/while/body/eval_jaxpr/ppermute | solution.py:13
  110.3 11.5 %collective-permute-start = (bf16[512,256]{1,0:T(8,128)(2,1)S(1)}, bf16[512,256]{1,0:T(8,128)(2,1)S(1)}, u32[]{:S(2)}, u32[]{:S(2)}) collective-permute-start(bf16[512,256]{1,0:T(8,128)(2,1)S(1)} %get-tuple-element.291), channel_id=1, source_target_pairs={{0,2},{2,4},{4,6},{6,8},{8,10},{10,12},{12,14},{14,16},{16,18},{18... | collective-permute-start | bytes 786440 | tf_op jit(solution)/shard_map/while/body/eval_jaxpr/ppermute | solution.py:13
  122.5 11.5 %collective-permute-start = (bf16[512,256]{1,0:T(8,128)(2,1)S(1)}, bf16[512,256]{1,0:T(8,128)(2,1)S(1)}, u32[]{:S(2)}, u32[]{:S(2)}) collective-permute-start(bf16[512,256]{1,0:T(8,128)(2,1)S(1)} %get-tuple-element.291), channel_id=1, source_target_pairs={{0,2},{2,4},{4,6},{6,8},{8,10},{10,12},{12,14},{14,16},{16,18},{18... | collective-permute-start | bytes 786440 | tf_op jit(solution)/shard_map/while/body/eval_jaxpr/ppermute | solution.py:13
  134.8 11.5 %collective-permute-start = (bf16[512,256]{1,0:T(8,128)(2,1)S(1)}, bf16[512,256]{1,0:T(8,128)(2,1)S(1)}, u32[]{:S(2)}, u32[]{:S(2)}) collective-permute-start(bf16[512,256]{1,0:T(8,128)(2,1)S(1)} %get-tuple-element.291), channel_id=1, source_target_pairs={{0,2},{2,4},{4,6},{6,8},{8,10},{10,12},{12,14},{14,16},{16,18},{18... | collective-permute-start | bytes 786440 | tf_op jit(solution)/shard_map/while/body/eval_jaxpr/ppermute | solution.py:13
  147.1 11.5 %collective-permute-start = (bf16[512,256]{1,0:T(8,128)(2,1)S(1)}, bf16[512,256]{1,0:T(8,128)(2,1)S(1)}, u32[]{:S(2)}, u32[]{:S(2)}) collective-permute-start(bf16[512,256]{1,0:T(8,128)(2,1)S(1)} %get-tuple-element.291), channel_id=1, source_target_pairs={{0,2},{2,4},{4,6},{6,8},{8,10},{10,12},{12,14},{14,16},{16,18},{18... | collective-permute-start | bytes 786440 | tf_op jit(solution)/shard_map/while/body/eval_jaxpr/ppermute | solution.py:13
  159.3 11.5 %collective-permute-start = (bf16[512,256]{1,0:T(8,128)(2,1)S(1)}, bf16[512,256]{1,0:T(8,128)(2,1)S(1)}, u32[]{:S(2)}, u32[]{:S(2)}) collective-permute-start(bf16[512,256]{1,0:T(8,128)(2,1)S(1)} %get-tuple-element.291), channel_id=1, source_target_pairs={{0,2},{2,4},{4,6},{6,8},{8,10},{10,12},{12,14},{14,16},{16,18},{18... | collective-permute-start | bytes 786440 | tf_op jit(solution)/shard_map/while/body/eval_jaxpr/ppermute | solution.py:13
  171.6 11.5 %collective-permute-start = (bf16[512,256]{1,0:T(8,128)(2,1)S(1)}, bf16[512,256]{1,0:T(8,128)(2,1)S(1)}, u32[]{:S(2)}, u32[]{:S(2)}) collective-permute-start(bf16[512,256]{1,0:T(8,128)(2,1)S(1)} %get-tuple-element.291), channel_id=1, source_target_pairs={{0,2},{2,4},{4,6},{6,8},{8,10},{10,12},{12,14},{14,16},{16,18},{18... | collective-permute-start | bytes 786440 | tf_op jit(solution)/shard_map/while/body/eval_jaxpr/ppermute | solution.py:13
  183.9 11.5 %collective-permute-start = (bf16[512,256]{1,0:T(8,128)(2,1)S(1)}, bf16[512,256]{1,0:T(8,128)(2,1)S(1)}, u32[]{:S(2)}, u32[]{:S(2)}) collective-permute-start(bf16[512,256]{1,0:T(8,128)(2,1)S(1)} %get-tuple-element.291), channel_id=1, source_target_pairs={{0,2},{2,4},{4,6},{6,8},{8,10},{10,12},{12,14},{14,16},{16,18},{18... | collective-permute-start | bytes 786440 | tf_op jit(solution)/shard_map/while/body/eval_jaxpr/ppermute | solution.py:13
  196.2 11.5 %collective-permute-start = (bf16[512,256]{1,0:T(8,128)(2,1)S(1)}, bf16[512,256]{1,0:T(8,128)(2,1)S(1)}, u32[]{:S(2)}, u32[]{:S(2)}) collective-permute-start(bf16[512,256]{1,0:T(8,128)(2,1)S(1)} %get-tuple-element.291), channel_id=1, source_target_pairs={{0,2},{2,4},{4,6},{6,8},{8,10},{10,12},{12,14},{14,16},{16,18},{18... | collective-permute-start | bytes 786440 | tf_op jit(solution)/shard_map/while/body/eval_jaxpr/ppermute | solution.py:13
  208.5 11.5 %collective-permute-start = (bf16[512,256]{1,0:T(8,128)(2,1)S(1)}, bf16[512,256]{1,0:T(8,128)(2,1)S(1)}, u32[]{:S(2)}, u32[]{:S(2)}) collective-permute-start(bf16[512,256]{1,0:T(8,128)(2,1)S(1)} %get-tuple-element.291), channel_id=1, source_target_pairs={{0,2},{2,4},{4,6},{6,8},{8,10},{10,12},{12,14},{14,16},{16,18},{18... | collective-permute-start | bytes 786440 | tf_op jit(solution)/shard_map/while/body/eval_jaxpr/ppermute | solution.py:13
  220.8 11.5 %collective-permute-start = (bf16[512,256]{1,0:T(8,128)(2,1)S(1)}, bf16[512,256]{1,0:T(8,128)(2,1)S(1)}, u32[]{:S(2)}, u32[]{:S(2)}) collective-permute-start(bf16[512,256]{1,0:T(8,128)(2,1)S(1)} %get-tuple-element.291), channel_id=1, source_target_pairs={{0,2},{2,4},{4,6},{6,8},{8,10},{10,12},{12,14},{14,16},{16,18},{18... | collective-permute-start | bytes 786440 | tf_op jit(solution)/shard_map/while/body/eval_jaxpr/ppermute | solution.py:13
  233.0 11.5 %collective-permute-start = (bf16[512,256]{1,0:T(8,128)(2,1)S(1)}, bf16[512,256]{1,0:T(8,128)(2,1)S(1)}, u32[]{:S(2)}, u32[]{:S(2)}) collective-permute-start(bf16[512,256]{1,0:T(8,128)(2,1)S(1)} %get-tuple-element.291), channel_id=1, source_target_pairs={{0,2},{2,4},{4,6},{6,8},{8,10},{10,12},{12,14},{14,16},{16,18},{18... | collective-permute-start | bytes 786440 | tf_op jit(solution)/shard_map/while/body/eval_jaxpr/ppermute | solution.py:13
  245.3 11.5 %collective-permute-start = (bf16[512,256]{1,0:T(8,128)(2,1)S(1)}, bf16[512,256]{1,0:T(8,128)(2,1)S(1)}, u32[]{:S(2)}, u32[]{:S(2)}) collective-permute-start(bf16[512,256]{1,0:T(8,128)(2,1)S(1)} %get-tuple-element.291), channel_id=1, source_target_pairs={{0,2},{2,4},{4,6},{6,8},{8,10},{10,12},{12,14},{14,16},{16,18},{18... | collective-permute-start | bytes 786440 | tf_op jit(solution)/shard_map/while/body/eval_jaxpr/ppermute | solution.py:13
  257.6 11.5 %collective-permute-start = (bf16[512,256]{1,0:T(8,128)(2,1)S(1)}, bf16[512,256]{1,0:T(8,128)(2,1)S(1)}, u32[]{:S(2)}, u32[]{:S(2)}) collective-permute-start(bf16[512,256]{1,0:T(8,128)(2,1)S(1)} %get-tuple-element.291), channel_id=1, source_target_pairs={{0,2},{2,4},{4,6},{6,8},{8,10},{10,12},{12,14},{14,16},{16,18},{18... | collective-permute-start | bytes 786440 | tf_op jit(solution)/shard_map/while/body/eval_jaxpr/ppermute | solution.py:13
  269.8 11.5 %collective-permute-start = (bf16[512,256]{1,0:T(8,128)(2,1)S(1)}, bf16[512,256]{1,0:T(8,128)(2,1)S(1)}, u32[]{:S(2)}, u32[]{:S(2)}) collective-permute-start(bf16[512,256]{1,0:T(8,128)(2,1)S(1)} %get-tuple-element.291), channel_id=1, source_target_pairs={{0,2},{2,4},{4,6},{6,8},{8,10},{10,12},{12,14},{14,16},{16,18},{18... | collective-permute-start | bytes 786440 | tf_op jit(solution)/shard_map/while/body/eval_jaxpr/ppermute | solution.py:13
  282.1 11.5 %collective-permute-start = (bf16[512,256]{1,0:T(8,128)(2,1)S(1)}, bf16[512,256]{1,0:T(8,128)(2,1)S(1)}, u32[]{:S(2)}, u32[]{:S(2)}) collective-permute-start(bf16[512,256]{1,0:T(8,128)(2,1)S(1)} %get-tuple-element.291), channel_id=1, source_target_pairs={{0,2},{2,4},{4,6},{6,8},{8,10},{10,12},{12,14},{14,16},{16,18},{18... | collective-permute-start | bytes 786440 | tf_op jit(solution)/shard_map/while/body/eval_jaxpr/ppermute | solution.py:13
  294.4 11.5 %collective-permute-start = (bf16[512,256]{1,0:T(8,128)(2,1)S(1)}, bf16[512,256]{1,0:T(8,128)(2,1)S(1)}, u32[]{:S(2)}, u32[]{:S(2)}) collective-permute-start(bf16[512,256]{1,0:T(8,128)(2,1)S(1)} %get-tuple-element.291), channel_id=1, source_target_pairs={{0,2},{2,4},{4,6},{6,8},{8,10},{10,12},{12,14},{14,16},{16,18},{18... | collective-permute-start | bytes 786440 | tf_op jit(solution)/shard_map/while/body/eval_jaxpr/ppermute | solution.py:13
  306.6 11.5 %collective-permute-start = (bf16[512,256]{1,0:T(8,128)(2,1)S(1)}, bf16[512,256]{1,0:T(8,128)(2,1)S(1)}, u32[]{:S(2)}, u32[]{:S(2)}) collective-permute-start(bf16[512,256]{1,0:T(8,128)(2,1)S(1)} %get-tuple-element.291), channel_id=1, source_target_pairs={{0,2},{2,4},{4,6},{6,8},{8,10},{10,12},{12,14},{14,16},{16,18},{18... | collective-permute-start | bytes 786440 | tf_op jit(solution)/shard_map/while/body/eval_jaxpr/ppermute | solution.py:13
  318.9 11.5 %collective-permute-start = (bf16[512,256]{1,0:T(8,128)(2,1)S(1)}, bf16[512,256]{1,0:T(8,128)(2,1)S(1)}, u32[]{:S(2)}, u32[]{:S(2)}) collective-permute-start(bf16[512,256]{1,0:T(8,128)(2,1)S(1)} %get-tuple-element.291), channel_id=1, source_target_pairs={{0,2},{2,4},{4,6},{6,8},{8,10},{10,12},{12,14},{14,16},{16,18},{18... | collective-permute-start | bytes 786440 | tf_op jit(solution)/shard_map/while/body/eval_jaxpr/ppermute | solution.py:13
  331.2 11.5 %collective-permute-start = (bf16[512,256]{1,0:T(8,128)(2,1)S(1)}, bf16[512,256]{1,0:T(8,128)(2,1)S(1)}, u32[]{:S(2)}, u32[]{:S(2)}) collective-permute-start(bf16[512,256]{1,0:T(8,128)(2,1)S(1)} %get-tuple-element.291), channel_id=1, source_target_pairs={{0,2},{2,4},{4,6},{6,8},{8,10},{10,12},{12,14},{14,16},{16,18},{18... | collective-permute-start | bytes 786440 | tf_op jit(solution)/shard_map/while/body/eval_jaxpr/ppermute | solution.py:13
  343.4 11.5 %collective-permute-start = (bf16[512,256]{1,0:T(8,128)(2,1)S(1)}, bf16[512,256]{1,0:T(8,128)(2,1)S(1)}, u32[]{:S(2)}, u32[]{:S(2)}) collective-permute-start(bf16[512,256]{1,0:T(8,128)(2,1)S(1)} %get-tuple-element.291), channel_id=1, source_target_pairs={{0,2},{2,4},{4,6},{6,8},{8,10},{10,12},{12,14},{14,16},{16,18},{18... | collective-permute-start | bytes 786440 | tf_op jit(solution)/shard_map/while/body/eval_jaxpr/ppermute | solution.py:13
  355.7 11.6 %collective-permute-start = (bf16[512,256]{1,0:T(8,128)(2,1)S(1)}, bf16[512,256]{1,0:T(8,128)(2,1)S(1)}, u32[]{:S(2)}, u32[]{:S(2)}) collective-permute-start(bf16[512,256]{1,0:T(8,128)(2,1)S(1)} %get-tuple-element.291), channel_id=1, source_target_pairs={{0,2},{2,4},{4,6},{6,8},{8,10},{10,12},{12,14},{14,16},{16,18},{18... | collective-permute-start | bytes 786440 | tf_op jit(solution)/shard_map/while/body/eval_jaxpr/ppermute | solution.py:13
  368.0 11.5 %collective-permute-start = (bf16[512,256]{1,0:T(8,128)(2,1)S(1)}, bf16[512,256]{1,0:T(8,128)(2,1)S(1)}, u32[]{:S(2)}, u32[]{:S(2)}) collective-permute-start(bf16[512,256]{1,0:T(8,128)(2,1)S(1)} %get-tuple-element.291), channel_id=1, source_target_pairs={{0,2},{2,4},{4,6},{6,8},{8,10},{10,12},{12,14},{14,16},{16,18},{18... | collective-permute-start | bytes 786440 | tf_op jit(solution)/shard_map/while/body/eval_jaxpr/ppermute | solution.py:13
  380.3 11.5 %collective-permute-start = (bf16[512,256]{1,0:T(8,128)(2,1)S(1)}, bf16[512,256]{1,0:T(8,128)(2,1)S(1)}, u32[]{:S(2)}, u32[]{:S(2)}) collective-permute-start(bf16[512,256]{1,0:T(8,128)(2,1)S(1)} %get-tuple-element.291), channel_id=1, source_target_pairs={{0,2},{2,4},{4,6},{6,8},{8,10},{10,12},{12,14},{14,16},{16,18},{18... | collective-permute-start | bytes 786440 | tf_op jit(solution)/shard_map/while/body/eval_jaxpr/ppermute | solution.py:13
  392.6 11.5 %collective-permute-start = (bf16[512,256]{1,0:T(8,128)(2,1)S(1)}, bf16[512,256]{1,0:T(8,128)(2,1)S(1)}, u32[]{:S(2)}, u32[]{:S(2)}) collective-permute-start(bf16[512,256]{1,0:T(8,128)(2,1)S(1)} %get-tuple-element.291), channel_id=1, source_target_pairs={{0,2},{2,4},{4,6},{6,8},{8,10},{10,12},{12,14},{14,16},{16,18},{18... | collective-permute-start | bytes 786440 | tf_op jit(solution)/shard_map/while/body/eval_jaxpr/ppermute | solution.py:13
  404.9 11.5 %collective-permute-start = (bf16[512,256]{1,0:T(8,128)(2,1)S(1)}, bf16[512,256]{1,0:T(8,128)(2,1)S(1)}, u32[]{:S(2)}, u32[]{:S(2)}) collective-permute-start(bf16[512,256]{1,0:T(8,128)(2,1)S(1)} %get-tuple-element.291), channel_id=1, source_target_pairs={{0,2},{2,4},{4,6},{6,8},{8,10},{10,12},{12,14},{14,16},{16,18},{18... | collective-permute-start | bytes 786440 | tf_op jit(solution)/shard_map/while/body/eval_jaxpr/ppermute | solution.py:13
  417.2 11.5 %collective-permute-start = (bf16[512,256]{1,0:T(8,128)(2,1)S(1)}, bf16[512,256]{1,0:T(8,128)(2,1)S(1)}, u32[]{:S(2)}, u32[]{:S(2)}) collective-permute-start(bf16[512,256]{1,0:T(8,128)(2,1)S(1)} %get-tuple-element.291), channel_id=1, source_target_pairs={{0,2},{2,4},{4,6},{6,8},{8,10},{10,12},{12,14},{14,16},{16,18},{18... | collective-permute-start | bytes 786440 | tf_op jit(solution)/shard_map/while/body/eval_jaxpr/ppermute | solution.py:13
  429.4 11.5 %collective-permute-start = (bf16[512,256]{1,0:T(8,128)(2,1)S(1)}, bf16[512,256]{1,0:T(8,128)(2,1)S(1)}, u32[]{:S(2)}, u32[]{:S(2)}) collective-permute-start(bf16[512,256]{1,0:T(8,128)(2,1)S(1)} %get-tuple-element.291), channel_id=1, source_target_pairs={{0,2},{2,4},{4,6},{6,8},{8,10},{10,12},{12,14},{14,16},{16,18},{18... | collective-permute-start | bytes 786440 | tf_op jit(solution)/shard_map/while/body/eval_jaxpr/ppermute | solution.py:13
  441.7 11.5 %collective-permute-start = (bf16[512,256]{1,0:T(8,128)(2,1)S(1)}, bf16[512,256]{1,0:T(8,128)(2,1)S(1)}, u32[]{:S(2)}, u32[]{:S(2)}) collective-permute-start(bf16[512,256]{1,0:T(8,128)(2,1)S(1)} %get-tuple-element.291), channel_id=1, source_target_pairs={{0,2},{2,4},{4,6},{6,8},{8,10},{10,12},{12,14},{14,16},{16,18},{18... | collective-permute-start | bytes 786440 | tf_op jit(solution)/shard_map/while/body/eval_jaxpr/ppermute | solution.py:13
  454.0 11.5 %collective-permute-start = (bf16[512,256]{1,0:T(8,128)(2,1)S(1)}, bf16[512,256]{1,0:T(8,128)(2,1)S(1)}, u32[]{:S(2)}, u32[]{:S(2)}) collective-permute-start(bf16[512,256]{1,0:T(8,128)(2,1)S(1)} %get-tuple-element.291), channel_id=1, source_target_pairs={{0,2},{2,4},{4,6},{6,8},{8,10},{10,12},{12,14},{14,16},{16,18},{18... | collective-permute-start | bytes 786440 | tf_op jit(solution)/shard_map/while/body/eval_jaxpr/ppermute | solution.py:13
  466.3 11.5 %collective-permute-start = (bf16[512,256]{1,0:T(8,128)(2,1)S(1)}, bf16[512,256]{1,0:T(8,128)(2,1)S(1)}, u32[]{:S(2)}, u32[]{:S(2)}) collective-permute-start(bf16[512,256]{1,0:T(8,128)(2,1)S(1)} %get-tuple-element.291), channel_id=1, source_target_pairs={{0,2},{2,4},{4,6},{6,8},{8,10},{10,12},{12,14},{14,16},{16,18},{18... | collective-permute-start | bytes 786440 | tf_op jit(solution)/shard_map/while/body/eval_jaxpr/ppermute | solution.py:13
  478.5 11.5 %collective-permute-start = (bf16[512,256]{1,0:T(8,128)(2,1)S(1)}, bf16[512,256]{1,0:T(8,128)(2,1)S(1)}, u32[]{:S(2)}, u32[]{:S(2)}) collective-permute-start(bf16[512,256]{1,0:T(8,128)(2,1)S(1)} %get-tuple-element.291), channel_id=1, source_target_pairs={{0,2},{2,4},{4,6},{6,8},{8,10},{10,12},{12,14},{14,16},{16,18},{18... | collective-permute-start | bytes 786440 | tf_op jit(solution)/shard_map/while/body/eval_jaxpr/ppermute | solution.py:13
  490.8 11.5 %collective-permute-start = (bf16[512,256]{1,0:T(8,128)(2,1)S(1)}, bf16[512,256]{1,0:T(8,128)(2,1)S(1)}, u32[]{:S(2)}, u32[]{:S(2)}) collective-permute-start(bf16[512,256]{1,0:T(8,128)(2,1)S(1)} %get-tuple-element.291), channel_id=1, source_target_pairs={{0,2},{2,4},{4,6},{6,8},{8,10},{10,12},{12,14},{14,16},{16,18},{18... | collective-permute-start | bytes 786440 | tf_op jit(solution)/shard_map/while/body/eval_jaxpr/ppermute | solution.py:13
  503.0 11.5 %collective-permute-start = (bf16[512,256]{1,0:T(8,128)(2,1)S(1)}, bf16[512,256]{1,0:T(8,128)(2,1)S(1)}, u32[]{:S(2)}, u32[]{:S(2)}) collective-permute-start(bf16[512,256]{1,0:T(8,128)(2,1)S(1)} %get-tuple-element.291), channel_id=1, source_target_pairs={{0,2},{2,4},{4,6},{6,8},{8,10},{10,12},{12,14},{14,16},{16,18},{18... | collective-permute-start | bytes 786440 | tf_op jit(solution)/shard_map/while/body/eval_jaxpr/ppermute | solution.py:13
  515.3 11.5 %collective-permute-start = (bf16[512,256]{1,0:T(8,128)(2,1)S(1)}, bf16[512,256]{1,0:T(8,128)(2,1)S(1)}, u32[]{:S(2)}, u32[]{:S(2)}) collective-permute-start(bf16[512,256]{1,0:T(8,128)(2,1)S(1)} %get-tuple-element.291), channel_id=1, source_target_pairs={{0,2},{2,4},{4,6},{6,8},{8,10},{10,12},{12,14},{14,16},{16,18},{18... | collective-permute-start | bytes 786440 | tf_op jit(solution)/shard_map/while/body/eval_jaxpr/ppermute | solution.py:13
  527.6 11.5 %collective-permute-start = (bf16[512,256]{1,0:T(8,128)(2,1)S(1)}, bf16[512,256]{1,0:T(8,128)(2,1)S(1)}, u32[]{:S(2)}, u32[]{:S(2)}) collective-permute-start(bf16[512,256]{1,0:T(8,128)(2,1)S(1)} %get-tuple-element.291), channel_id=1, source_target_pairs={{0,2},{2,4},{4,6},{6,8},{8,10},{10,12},{12,14},{14,16},{16,18},{18... | collective-permute-start | bytes 786440 | tf_op jit(solution)/shard_map/while/body/eval_jaxpr/ppermute | solution.py:13
  539.9 11.5 %collective-permute-start = (bf16[512,256]{1,0:T(8,128)(2,1)S(1)}, bf16[512,256]{1,0:T(8,128)(2,1)S(1)}, u32[]{:S(2)}, u32[]{:S(2)}) collective-permute-start(bf16[512,256]{1,0:T(8,128)(2,1)S(1)} %get-tuple-element.291), channel_id=1, source_target_pairs={{0,2},{2,4},{4,6},{6,8},{8,10},{10,12},{12,14},{14,16},{16,18},{18... | collective-permute-start | bytes 786440 | tf_op jit(solution)/shard_map/while/body/eval_jaxpr/ppermute | solution.py:13
  552.1 11.5 %collective-permute-start = (bf16[512,256]{1,0:T(8,128)(2,1)S(1)}, bf16[512,256]{1,0:T(8,128)(2,1)S(1)}, u32[]{:S(2)}, u32[]{:S(2)}) collective-permute-start(bf16[512,256]{1,0:T(8,128)(2,1)S(1)} %get-tuple-element.291), channel_id=1, source_target_pairs={{0,2},{2,4},{4,6},{6,8},{8,10},{10,12},{12,14},{14,16},{16,18},{18... | collective-permute-start | bytes 786440 | tf_op jit(solution)/shard_map/while/body/eval_jaxpr/ppermute | solution.py:13
  564.4 11.5 %collective-permute-start = (bf16[512,256]{1,0:T(8,128)(2,1)S(1)}, bf16[512,256]{1,0:T(8,128)(2,1)S(1)}, u32[]{:S(2)}, u32[]{:S(2)}) collective-permute-start(bf16[512,256]{1,0:T(8,128)(2,1)S(1)} %get-tuple-element.291), channel_id=1, source_target_pairs={{0,2},{2,4},{4,6},{6,8},{8,10},{10,12},{12,14},{14,16},{16,18},{18... | collective-permute-start | bytes 786440 | tf_op jit(solution)/shard_map/while/body/eval_jaxpr/ppermute | solution.py:13
  576.7 11.5 %collective-permute-start = (bf16[512,256]{1,0:T(8,128)(2,1)S(1)}, bf16[512,256]{1,0:T(8,128)(2,1)S(1)}, u32[]{:S(2)}, u32[]{:S(2)}) collective-permute-start(bf16[512,256]{1,0:T(8,128)(2,1)S(1)} %get-tuple-element.291), channel_id=1, source_target_pairs={{0,2},{2,4},{4,6},{6,8},{8,10},{10,12},{12,14},{14,16},{16,18},{18... | collective-permute-start | bytes 786440 | tf_op jit(solution)/shard_map/while/body/eval_jaxpr/ppermute | solution.py:13
  589.0 11.5 %collective-permute-start = (bf16[512,256]{1,0:T(8,128)(2,1)S(1)}, bf16[512,256]{1,0:T(8,128)(2,1)S(1)}, u32[]{:S(2)}, u32[]{:S(2)}) collective-permute-start(bf16[512,256]{1,0:T(8,128)(2,1)S(1)} %get-tuple-element.291), channel_id=1, source_target_pairs={{0,2},{2,4},{4,6},{6,8},{8,10},{10,12},{12,14},{14,16},{16,18},{18... | collective-permute-start | bytes 786440 | tf_op jit(solution)/shard_map/while/body/eval_jaxpr/ppermute | solution.py:13
  601.3 11.5 %collective-permute-start = (bf16[512,256]{1,0:T(8,128)(2,1)S(1)}, bf16[512,256]{1,0:T(8,128)(2,1)S(1)}, u32[]{:S(2)}, u32[]{:S(2)}) collective-permute-start(bf16[512,256]{1,0:T(8,128)(2,1)S(1)} %get-tuple-element.291), channel_id=1, source_target_pairs={{0,2},{2,4},{4,6},{6,8},{8,10},{10,12},{12,14},{14,16},{16,18},{18... | collective-permute-start | bytes 786440 | tf_op jit(solution)/shard_map/while/body/eval_jaxpr/ppermute | solution.py:13
  613.5 11.5 %collective-permute-start = (bf16[512,256]{1,0:T(8,128)(2,1)S(1)}, bf16[512,256]{1,0:T(8,128)(2,1)S(1)}, u32[]{:S(2)}, u32[]{:S(2)}) collective-permute-start(bf16[512,256]{1,0:T(8,128)(2,1)S(1)} %get-tuple-element.291), channel_id=1, source_target_pairs={{0,2},{2,4},{4,6},{6,8},{8,10},{10,12},{12,14},{14,16},{16,18},{18... | collective-permute-start | bytes 786440 | tf_op jit(solution)/shard_map/while/body/eval_jaxpr/ppermute | solution.py:13
  625.8 11.5 %collective-permute-start = (bf16[512,256]{1,0:T(8,128)(2,1)S(1)}, bf16[512,256]{1,0:T(8,128)(2,1)S(1)}, u32[]{:S(2)}, u32[]{:S(2)}) collective-permute-start(bf16[512,256]{1,0:T(8,128)(2,1)S(1)} %get-tuple-element.291), channel_id=1, source_target_pairs={{0,2},{2,4},{4,6},{6,8},{8,10},{10,12},{12,14},{14,16},{16,18},{18... | collective-permute-start | bytes 786440 | tf_op jit(solution)/shard_map/while/body/eval_jaxpr/ppermute | solution.py:13
  638.0 11.5 %collective-permute-start = (bf16[512,256]{1,0:T(8,128)(2,1)S(1)}, bf16[512,256]{1,0:T(8,128)(2,1)S(1)}, u32[]{:S(2)}, u32[]{:S(2)}) collective-permute-start(bf16[512,256]{1,0:T(8,128)(2,1)S(1)} %get-tuple-element.291), channel_id=1, source_target_pairs={{0,2},{2,4},{4,6},{6,8},{8,10},{10,12},{12,14},{14,16},{16,18},{18... | collective-permute-start | bytes 786440 | tf_op jit(solution)/shard_map/while/body/eval_jaxpr/ppermute | solution.py:13
  650.3 11.5 %collective-permute-start = (bf16[512,256]{1,0:T(8,128)(2,1)S(1)}, bf16[512,256]{1,0:T(8,128)(2,1)S(1)}, u32[]{:S(2)}, u32[]{:S(2)}) collective-permute-start(bf16[512,256]{1,0:T(8,128)(2,1)S(1)} %get-tuple-element.291), channel_id=1, source_target_pairs={{0,2},{2,4},{4,6},{6,8},{8,10},{10,12},{12,14},{14,16},{16,18},{18... | collective-permute-start | bytes 786440 | tf_op jit(solution)/shard_map/while/body/eval_jaxpr/ppermute | solution.py:13
  662.6 11.5 %collective-permute-start = (bf16[512,256]{1,0:T(8,128)(2,1)S(1)}, bf16[512,256]{1,0:T(8,128)(2,1)S(1)}, u32[]{:S(2)}, u32[]{:S(2)}) collective-permute-start(bf16[512,256]{1,0:T(8,128)(2,1)S(1)} %get-tuple-element.291), channel_id=1, source_target_pairs={{0,2},{2,4},{4,6},{6,8},{8,10},{10,12},{12,14},{14,16},{16,18},{18... | collective-permute-start | bytes 786440 | tf_op jit(solution)/shard_map/while/body/eval_jaxpr/ppermute | solution.py:13
  674.9 11.5 %collective-permute-start = (bf16[512,256]{1,0:T(8,128)(2,1)S(1)}, bf16[512,256]{1,0:T(8,128)(2,1)S(1)}, u32[]{:S(2)}, u32[]{:S(2)}) collective-permute-start(bf16[512,256]{1,0:T(8,128)(2,1)S(1)} %get-tuple-element.291), channel_id=1, source_target_pairs={{0,2},{2,4},{4,6},{6,8},{8,10},{10,12},{12,14},{14,16},{16,18},{18... | collective-permute-start | bytes 786440 | tf_op jit(solution)/shard_map/while/body/eval_jaxpr/ppermute | solution.py:13
  687.2 11.5 %collective-permute-start = (bf16[512,256]{1,0:T(8,128)(2,1)S(1)}, bf16[512,256]{1,0:T(8,128)(2,1)S(1)}, u32[]{:S(2)}, u32[]{:S(2)}) collective-permute-start(bf16[512,256]{1,0:T(8,128)(2,1)S(1)} %get-tuple-element.291), channel_id=1, source_target_pairs={{0,2},{2,4},{4,6},{6,8},{8,10},{10,12},{12,14},{14,16},{16,18},{18... | collective-permute-start | bytes 786440 | tf_op jit(solution)/shard_map/while/body/eval_jaxpr/ppermute | solution.py:13
  699.4 11.5 %collective-permute-start = (bf16[512,256]{1,0:T(8,128)(2,1)S(1)}, bf16[512,256]{1,0:T(8,128)(2,1)S(1)}, u32[]{:S(2)}, u32[]{:S(2)}) collective-permute-start(bf16[512,256]{1,0:T(8,128)(2,1)S(1)} %get-tuple-element.291), channel_id=1, source_target_pairs={{0,2},{2,4},{4,6},{6,8},{8,10},{10,12},{12,14},{14,16},{16,18},{18... | collective-permute-start | bytes 786440 | tf_op jit(solution)/shard_map/while/body/eval_jaxpr/ppermute | solution.py:13
  711.7 11.5 %collective-permute-start = (bf16[512,256]{1,0:T(8,128)(2,1)S(1)}, bf16[512,256]{1,0:T(8,128)(2,1)S(1)}, u32[]{:S(2)}, u32[]{:S(2)}) collective-permute-start(bf16[512,256]{1,0:T(8,128)(2,1)S(1)} %get-tuple-element.291), channel_id=1, source_target_pairs={{0,2},{2,4},{4,6},{6,8},{8,10},{10,12},{12,14},{14,16},{16,18},{18... | collective-permute-start | bytes 786440 | tf_op jit(solution)/shard_map/while/body/eval_jaxpr/ppermute | solution.py:13
  723.9 11.5 %collective-permute-start = (bf16[512,256]{1,0:T(8,128)(2,1)S(1)}, bf16[512,256]{1,0:T(8,128)(2,1)S(1)}, u32[]{:S(2)}, u32[]{:S(2)}) collective-permute-start(bf16[512,256]{1,0:T(8,128)(2,1)S(1)} %get-tuple-element.291), channel_id=1, source_target_pairs={{0,2},{2,4},{4,6},{6,8},{8,10},{10,12},{12,14},{14,16},{16,18},{18... | collective-permute-start | bytes 786440 | tf_op jit(solution)/shard_map/while/body/eval_jaxpr/ppermute | solution.py:13
  736.2 11.5 %collective-permute-start = (bf16[512,256]{1,0:T(8,128)(2,1)S(1)}, bf16[512,256]{1,0:T(8,128)(2,1)S(1)}, u32[]{:S(2)}, u32[]{:S(2)}) collective-permute-start(bf16[512,256]{1,0:T(8,128)(2,1)S(1)} %get-tuple-element.291), channel_id=1, source_target_pairs={{0,2},{2,4},{4,6},{6,8},{8,10},{10,12},{12,14},{14,16},{16,18},{18... | collective-permute-start | bytes 786440 | tf_op jit(solution)/shard_map/while/body/eval_jaxpr/ppermute | solution.py:13
  748.5 11.5 %collective-permute-start = (bf16[512,256]{1,0:T(8,128)(2,1)S(1)}, bf16[512,256]{1,0:T(8,128)(2,1)S(1)}, u32[]{:S(2)}, u32[]{:S(2)}) collective-permute-start(bf16[512,256]{1,0:T(8,128)(2,1)S(1)} %get-tuple-element.291), channel_id=1, source_target_pairs={{0,2},{2,4},{4,6},{6,8},{8,10},{10,12},{12,14},{14,16},{16,18},{18... | collective-permute-start | bytes 786440 | tf_op jit(solution)/shard_map/while/body/eval_jaxpr/ppermute | solution.py:13
  760.7 11.5 %collective-permute-start = (bf16[512,256]{1,0:T(8,128)(2,1)S(1)}, bf16[512,256]{1,0:T(8,128)(2,1)S(1)}, u32[]{:S(2)}, u32[]{:S(2)}) collective-permute-start(bf16[512,256]{1,0:T(8,128)(2,1)S(1)} %get-tuple-element.291), channel_id=1, source_target_pairs={{0,2},{2,4},{4,6},{6,8},{8,10},{10,12},{12,14},{14,16},{16,18},{18... | collective-permute-start | bytes 786440 | tf_op jit(solution)/shard_map/while/body/eval_jaxpr/ppermute | solution.py:13
  (4 other events, 1550.6 us)
where the time goes:
time: 1100 us; the launch traced here: 1090 us
  waiting for transfers between devices  712 us (65%)
  matrix products  174 us (16%)
  local copies, waits for them, and re-layouts  159 us (14%)
  other arithmetic  26.6 us (2%)
  blocking collectives  11.8 us (1%)
    ppermute x63, waiting for transfers between devices, passed_along(): return lax.ppermute(value, axis, pairs)  712 us
    dot_general x16, matrix products, absorb(): jnp.einsum('kn,kif->nif', selector, products, precision=lax.Precision.HIG...  107 us
    gather x16, local copies, waits for them, and re-layouts, absorb(): picked = jnp.take(node_tiles, sources, axis=0)  103 us
    dot_general x16, matrix products, absorb(): jnp.einsum('kij,kjf->kif', matrices, picked, preferred_element_type=jnp.f...  63.2 us
    dynamic_update_slice x63, local copies, waits for them, and re-layouts, place(): return lax.dynamic_update_slice_in_dim(buffer, visitor, block_id * rows, 0)  46 us
    reduce_sum x16, other arithmetic, absorb(): row_sums = jnp.sum(matrices, axis=2, dtype=jnp.float32)  25.2 us
  transfers between devices with their start and end apart: 63, of which 63 were waited for; matrix products, arithmetic and copies ran while one was open for 0% of the time, Pallas kernels for 0%

commit v1 on v0

v1 whole, which is shorter than its diff:
```python
import functools

import jax
import jax.numpy as jnp
import numpy as np
from jax import lax
from jax.experimental import pallas as pl
from jax.experimental.pallas import tpu as pltpu
from jax.sharding import PartitionSpec as P

F = 512
TILE = 128
NTD = 4
EXTENT = (4, 2, 4, 2, 2)
VMEM_LIMIT = 8 * 2**20
TOGETHER = 4
HINT = 40


def coordinates():
    return [tuple(int(v) for v in c) for c in np.ndindex(*EXTENT)]


def linear(c):
    return int(np.ravel_multi_index(tuple(v % e for v, e in zip(c, EXTENT)), EXTENT))


class Piece:
    def __init__(self, value, tiles):
        self.value = value
        self.tiles = tiles

    def rows(self, begin, end):
        value = None if self.value is None else self.value[begin * TILE : end * TILE]
        return Piece(value, self.tiles[:, begin:end])

    def halves(self):
        count = self.tiles.shape[1]
        return self.rows(0, count // 2), self.rows(count // 2, count)


def join(*pieces):
    planned = pieces[0].value is None
    return Piece(
        None if planned else jnp.concatenate([p.value for p in pieces], axis=0),
        np.concatenate([p.tiles for p in pieces], axis=1),
    )


def moved(piece, where):
    pairs = [(linear(c), linear(where(*c))) for c in coordinates()]
    tiles = np.empty_like(piece.tiles)
    for source, target in pairs:
        tiles[target] = piece.tiles[source]
    value = piece.value
    if value is not None:
        value = lax.ppermute(value, ("blk", "rep"), pairs)
    return Piece(value, tiles)


def first_axis(piece, steps):
    return moved(
        piece,
        lambda y, h, x, c, z: (y, h, x + steps, c, z) if c == 0 else (y + steps, h, x, c, z),
    )


def second_axis(piece, steps):
    return moved(
        piece,
        lambda y, h, x, c, z: (y + steps, h, x, c, z) if c == 0 else (y, h, x + steps, c, z),
    )


def over_z(piece):
    return moved(piece, lambda y, h, x, c, z: (y, h + 1, x, c, z))


def other_core(piece):
    return moved(piece, lambda y, h, x, c, z: (y, h, x, 1 - c, z))


def after(piece, others):
    if piece.value is None:
        return piece
    return Piece(lax.optimization_barrier((piece.value, *others))[0], piece.tiles)


def plan(mine, absorb):
    plus, minus, over = (first_axis(mine, s) for s in (1, -1, 2))
    z_mine = over_z(mine)
    z_pair = over_z(join(plus, minus))
    near = join(mine, plus, minus, over, z_mine)
    near_up, near_down = second_axis(near, 1), second_axis(near, -1)
    z_over = first_axis(z_mine, 2)
    absorb([near, other_core(near)])
    far = join(z_pair, z_over)
    far_up = second_axis(join(far, near_up.rows(0, 3 * NTD)), 1)
    far_down = second_axis(join(far, near_down.rows(3 * NTD, 5 * NTD)), -1)
    absorb([near_up, near_down, other_core(near_up), other_core(near_down)])
    done = absorb([far, other_core(far)])
    end = join(
        second_axis(after(far_up.rows(0, NTD), (done,)), 1),
        second_axis(after(far_down.rows(NTD, 3 * NTD), (done,)), -1),
    )
    absorb([far_up, far_down])
    absorb([other_core(far_up), other_core(far_down)])
    absorb([end, other_core(end)], True)


def start_kernel(side_ref, codes_hbm, scales_hbm, weight_hbm, features_ref, weights_ref, codes_ref, scales_ref, sems):
    rows, half = codes_ref.shape
    groups = scales_ref.shape[0]
    width = half // groups
    cols = weights_ref.shape[2]
    side = side_ref[0]
    inputs = [
        pltpu.make_async_copy(codes_hbm, codes_ref, sems.at[0]),
        pltpu.make_async_copy(scales_hbm, scales_ref, sems.at[1]),
    ]
    for n in range(4):
        whose = side if n % 2 == 0 else 1 - side
        at = pl.ds(pl.multiple_of((n // 2) * F + whose * half, half), half)
        from_here = weight_hbm.at[at, pl.ds(pl.multiple_of(side * cols, cols), cols)]
        inputs.append(pltpu.make_async_copy(from_here, weights_ref.at[n], sems.at[2 + n]))
    for copy in inputs:
        copy.start()
    for copy in inputs[:2]:
        copy.wait()
    for g in range(groups):
        at = slice(g * width, (g + 1) * width)
        scales = jnp.broadcast_to(scales_ref[g : g + 1, :], (width, rows)).T
        scaled = codes_ref[:, at].astype(jnp.float32) * scales
        features_ref[:, at] = scaled.astype(features_ref.dtype)
    for copy in inputs[2:]:
        copy.wait()


def start(side, codes, scales, weight, cols):
    rows, half = codes.shape
    there = pl.BlockSpec(memory_space=pl.ANY)
    whole = pl.BlockSpec(memory_space=pltpu.VMEM)
    scales = scales.T
    far = [pltpu.with_memory_space_constraint(x, pltpu.HBM) for x in (codes, scales, weight)]
    return pl.pallas_call(
        start_kernel,
        in_specs=[pl.BlockSpec(memory_space=pltpu.SMEM)] + [there] * 3,
        out_specs=[whole, whole],
        out_shape=[pltpu.VMEM((rows, half), codes.dtype), pltpu.VMEM((4, half, cols), weight.dtype)],
        scratch_shapes=[
            pltpu.VMEM((rows, half), codes.dtype),
            pltpu.VMEM(scales.shape, scales.dtype),
            pltpu.SemaphoreType.DMA((6,)),
        ],
        compiler_params=pltpu.CompilerParams(vmem_limit_bytes=VMEM_LIMIT),
        name="start",
    )(side[None], *far)


def mix_kernel(first, features_ref, across_ref, weights_ref, *refs):
    out_ref = refs[-1]
    mixed = jnp.dot(features_ref[...], weights_ref[first], preferred_element_type=jnp.float32)
    mixed += jnp.dot(across_ref[...], weights_ref[first + 1], preferred_element_type=jnp.float32)
    for bias_ref in refs[:-1]:
        mixed += bias_ref[...]
    out_ref[...] = mixed.astype(out_ref.dtype)


def mix(first, features, across, weights, dtype, *bias):
    whole = pl.BlockSpec(memory_space=pltpu.VMEM)
    return pl.pallas_call(
        functools.partial(mix_kernel, first),
        in_specs=[whole] * (3 + len(bias)),
        out_specs=whole,
        out_shape=pltpu.VMEM((features.shape[0], weights.shape[2]), dtype),
        compiler_params=pltpu.CompilerParams(vmem_limit_bytes=VMEM_LIMIT),
        name="mix",
    )(features, across, weights, *bias)


def load_kernel(
    parts,
    device_ref,
    spots_hbm,
    source_hbm,
    target_hbm,
    adjacency_hbm,
    tiles_ref,
    lanes_ref,
    table_ref,
    spots_ref,
    source_ref,
    target_ref,
    sems,
):
    count = adjacency_hbm.shape[0]
    step = count // parts

    def copy(i):
        at = pl.ds(i * step, step)
        return pltpu.make_async_copy(adjacency_hbm.at[at], tiles_ref.at[at], sems.at[i])

    scalars = [
        pltpu.make_async_copy(spots_hbm.at[device_ref[0]], spots_ref, sems.at[parts]),
        pltpu.make_async_copy(source_hbm, source_ref, sems.at[parts + 1]),
        pltpu.make_async_copy(target_hbm, target_ref, sems.at[parts + 2]),
    ]
    for c in scalars:
        c.start()
    for i in range(parts):
        copy(i).start()
    tiles_ref[count] = jnp.zeros_like(tiles_ref[count])
    lanes_ref[...] = jnp.zeros_like(lanes_ref)

    def blank(k, carry):
        table_ref[k] = count
        return carry

    lax.fori_loop(0, table_ref.shape[0], blank, 0, unroll=16)
    for c in scalars:
        c.wait()

    def add(k, carry):
        target = target_ref[k]
        source = source_ref[k]
        table_ref[spots_ref[source // TILE, source % TILE] * NTD + target] = k
        lanes_ref[target] += tiles_ref[k].astype(jnp.float32)
        return carry

    for i in range(parts):
        copy(i).wait()
        lax.fori_loop(i * step, (i + 1) * step, add, 0, unroll=4)


def load(device, spots, adjacency, tile_source, tile_target):
    count = adjacency.shape[0]
    parts = 16
    there = pl.BlockSpec(memory_space=pl.ANY)
    whole = pl.BlockSpec(memory_space=pltpu.VMEM)
    scalars = pl.BlockSpec(memory_space=pltpu.SMEM)
    nodes = spots.shape[1]
    spots = jnp.asarray(spots.reshape(-1, nodes // TILE, TILE), jnp.int32)
    far = [
        pltpu.with_memory_space_constraint(x, pltpu.HBM)
        for x in (spots, tile_source, tile_target, adjacency)
    ]
    return pl.pallas_call(
        functools.partial(load_kernel, parts),
        in_specs=[scalars] + [there] * 4,
        out_specs=[whole, whole, scalars],
        out_shape=[
            pltpu.VMEM((count + 1, TILE, TILE), adjacency.dtype),
            pltpu.VMEM((NTD, TILE, TILE), jnp.float32),
            jax.ShapeDtypeStruct((nodes * NTD,), jnp.int32),
        ],
        scratch_shapes=[
            pltpu.SMEM((nodes // TILE, TILE), jnp.int32),
            pltpu.SMEM((count,), jnp.int32),
            pltpu.SMEM((count,), jnp.int32),
            pltpu.SemaphoreType.DMA((parts + 3,)),
        ],
        compiler_params=pltpu.CompilerParams(vmem_limit_bytes=VMEM_LIMIT),
        cost_estimate=pl.CostEstimate(
            flops=count * TILE * TILE, bytes_accessed=count * TILE * TILE * 2, transcendentals=0
        ),
        name="load",
    )(device[None], *far)


def gather_kernel(chunks, offset, first, last, table_ref, tiles_ref, *refs):
    pieces = refs[: len(chunks)]
    rest = refs[len(chunks) :]
    if last:
        total_in, lanes_ref, own_ref, out_ref, total = rest
        total[...] = total_in[...]
    elif first:
        (total,) = rest
        total[...] = jnp.zeros_like(total)
    else:
        total_in, total = rest
        total[...] = total_in[...]
    wide = NTD * TILE

    def product(piece, s, blocks, base):
        at = (base + s * NTD) * NTD

        def tile(t, j):
            return tiles_ref[table_ref[at + j * NTD + t]]

        left = jnp.concatenate(
            [
                jnp.concatenate([tile(t, j) for j in range(blocks * NTD)], axis=1)
                for t in range(NTD)
            ],
            axis=0,
        )
        right = piece[pl.ds(pl.multiple_of(s * wide, wide), blocks * wide)]
        return jnp.dot(left, right, preferred_element_type=jnp.float32)

    base = offset
    for piece, count in zip(pieces, chunks):

        def step(i, carry, piece=piece, base=base):
            total[...] += product(piece, i * TOGETHER, TOGETHER, base)
            return carry

        lax.fori_loop(0, count // TOGETHER, step, 0)
        if count % TOGETHER:
            total[...] += product(piece, count - count % TOGETHER, count % TOGETHER, base)
        base += count * NTD
    if last:
        degree = jnp.sum(lanes_ref[...], axis=1, keepdims=True)
        near = total[...] / jnp.sqrt(1.0 + degree)
        out_ref[...] = jnp.maximum(near + own_ref[...], 0.0).astype(out_ref.dtype)


def gathered(pieces, offset, table, tiles, width, total=None, ending=None):
    tiles = pltpu.with_memory_space_constraint(tiles, pltpu.VMEM)
    chunks = [p.value.shape[0] // (NTD * TILE) for p in pieces]
    wide = NTD * TILE
    whole = pl.BlockSpec(memory_space=pltpu.VMEM)
    scalars = pl.BlockSpec(memory_space=pltpu.SMEM)
    extra = ([] if total is None else [total]) + ([] if ending is None else list(ending))
    count = sum(chunks)
    last = ending is not None
    return pl.pallas_call(
        functools.partial(gather_kernel, chunks, offset, total is None, last),
        in_specs=[scalars, whole] + [whole] * (len(pieces) + len(extra)),
        out_specs=whole,
        out_shape=jax.ShapeDtypeStruct((wide, width), jnp.bfloat16 if last else jnp.float32),
        scratch_shapes=[pltpu.VMEM((wide, width), jnp.float32)] if last else [],
        compiler_params=pltpu.CompilerParams(vmem_limit_bytes=VMEM_LIMIT),
        cost_estimate=pl.CostEstimate(
            flops=HINT * count * wide * wide * width,
            bytes_accessed=count * wide * (wide + width),
            transcendentals=0,
        ),
        name="gather",
    )(table, tiles, *[p.value for p in pieces], *extra)


def body(feature_codes, group_scales, adjacency, tile_source, tile_target, weight, out_bias):
    cols = out_bias.shape[0]
    side = lax.axis_index("rep")
    device = lax.axis_index("blk") * 2 + side
    features, weights = start(side, feature_codes, group_scales, weight, cols)
    blocks = np.array([linear(c) // 2 for c in coordinates()])
    here = Piece(features, blocks[:, None] * NTD + np.arange(NTD)[None, :])
    across = moved(here, lambda y, h, x, c, z: (y, h, x, c, 1 - z))
    taken = []
    plan(Piece(None, here.tiles), lambda pieces, ending=False: taken.extend(p.tiles for p in pieces))
    order = np.concatenate(taken, axis=1)
    spots = np.argsort(order, axis=1)
    every = np.arange(lax.axis_size("blk") * NTD)
    assert np.array_equal(np.sort(order, axis=1), np.broadcast_to(every, order.shape))
    tiles, lanes, table = load(device, spots, adjacency, tile_source, tile_target)
    near, lanes = lax.optimization_barrier((across.value, lanes))
    lanes = lanes.reshape(NTD * TILE, TILE)
    sent = mix(2, features, near, weights, jnp.bfloat16)
    own = mix(0, features, near, weights, jnp.float32, out_bias[None])

    total = [None]
    place = [0]

    def absorb(pieces, ending=False):
        total[0] = gathered(
            pieces, place[0], table, tiles, cols, total[0], (lanes, own) if ending else None
        )
        place[0] += sum(p.tiles.shape[1] for p in pieces)
        return total[0]

    plan(Piece(sent, here.tiles), absorb)
    return total[0]


def solution(mesh):
    placed = (
        P("blk", "rep"),
        P("blk", "rep"),
        P("blk", None, None),
        P("blk"),
        P("blk"),
        P(),
        P("rep"),
    )
    return jax.shard_map(
        body, mesh=mesh, in_specs=placed, out_specs=P("blk", "rep"), check_vma=False
    )
```

time: 1100 us -> 85.1 us (0.08)
  waiting for transfers between devices: 712 us -> 25.6 us
  matrix products: 174 us -> 0 us
  local copies, waits for them, and re-layouts: 159 us -> 0.34 us
  starting transfers between devices: 5.31 us -> 35.3 us
  other arithmetic: 26.6 us -> 0.23 us
  Pallas kernels: 0 us -> 23.3 us
  blocking collectives: 11.8 us -> 0 us
    ppermute x63 -> x20, waiting for transfers between devices: 712 us -> 25.6 us  [moved(): value = lax.ppermute(value, ('blk', 'rep'), pairs)]
    dot_general x50 -> x0, matrix products: 174 us -> none  [the longest x16 107 us: absorb(): jnp.einsum('kn,kif->nif', selector, products, precision=lax.Precision.HIG...]
    gather x16 -> x0, local copies, waits for them, and re-layouts: 103 us -> none  [absorb(): picked = jnp.take(node_tiles, sources, axis=0)]
    dynamic_update_slice x63 -> x0, local copies, waits for them, and re-layouts: 46 us -> none  [place(): return lax.dynamic_update_slice_in_dim(buffer, visitor, block_id * rows, 0)]
    ppermute x63 -> x20, starting transfers between devices: 5.31 us -> 35.3 us  [moved(): value = lax.ppermute(value, ('blk', 'rep'), pairs)]
    reduce_sum x16 -> x0, other arithmetic: 25.2 us -> none  [absorb(): row_sums = jnp.sum(matrices, axis=2, dtype=jnp.float32)]
    pallas_call x0 -> x10, Pallas kernels: none -> 23.3 us  [the longest x6 13.9 us: gathered(): pl.pallas_call(functools.partial(gather_kernel, chunks, offset, total is...]
    all_gather x2 -> x0, blocking collectives: 11.8 us -> none  [the longest x1 5.9 us: body(): piece_near = lax.all_gather(neighbours, 'rep', axis=1, tiled=True)]
  transfers between devices with their start and end apart: 63 -> 20, of which waited for: 63 -> 9; matrix products, arithmetic and copies ran while one was open for 0% -> 1% of each run, Pallas kernels for 0% -> 23%
where the time goes in v1:
time: 85.1 us; the launch traced here: 85 us
  starting transfers between devices  35.3 us (41%)
  waiting for transfers between devices  25.6 us (30%)
  Pallas kernels  23.3 us (27%)
    ppermute x20, starting transfers between devices, moved(): value = lax.ppermute(value, ('blk', 'rep'), pairs)  35.3 us
    ppermute x20, waiting for transfers between devices, moved(): value = lax.ppermute(value, ('blk', 'rep'), pairs)  25.6 us
    pallas_call x6, Pallas kernels, gathered(): pl.pallas_call(functools.partial(gather_kernel, chunks, offset, total is...  13.9 us
    pallas_call x1, Pallas kernels, load(): pl.pallas_call(functools.partial(load_kernel, parts), in_specs=[scalars]...  7.58 us
  transfers between devices with their start and end apart: 20, of which 9 were waited for; matrix products, arithmetic and copies ran while one was open for 1% of the time, Pallas kernels for 23%

profile of v1, /device:TPU:1, one launch (start us, length us, event | category | flops | bytes accessed | tf_op | source)
XLA Modules:
  0.0 85.0 jit_solution(12259016661451851475)
XLA Ops:
  0.0 1.2 %start.1 = (bf16[512,256]{1,0:T(8,128)(2,1)S(1)}, bf16[4,256,256]{2,1,0:T(8,128)(2,1)S(1)}) custom-call(s32[1]{0:T(128)} %bitcast.1.side_ref, bf16[512,256]{1,0:T(8,128)(2,1)} %codes_hbm.1, f32[2,512]{1,0:T(2,128)} %bitcast.7, bf16[1024,512]{1,0:T(8,128)(2,1)} %weight_hbm.1), custom_call_target="tpu_custom_call" | custom-call | tf_op jit(solution)/shard_map/start/pallas_call | solution.py:145
  1.2 2.5 %collective-permute-start = (bf16[512,256]{1,0:T(8,128)(2,1)S(1)}, bf16[512,256]{1,0:T(8,128)(2,1)S(1)}, u32[]{:S(2)}, u32[]{:S(2)}) collective-permute-start(bf16[512,256]{1,0:T(8,128)(2,1)S(1)} %get-tuple-element.16.features_ref), channel_id=1, source_target_pairs={{0,1},{1,0},{2,3},{3,2},{4,5},{5,4},{6,7},{7,6},{8,9},{9,8},{10,11... | collective-permute-start | bytes 786440 | tf_op jit(solution)/shard_map/ppermute | solution.py:57
  3.8 7.6 %load.1 = (bf16[513,128,128]{2,1,0:T(8,128)(2,1)S(1)}, f32[4,128,128]{2,1,0:T(8,128)S(1)}, s32[1024]{0:T(1024)S(1)}) custom-call(s32[1]{0:T(128)} %bitcast.device_ref, s32[128,2,128]{2,1,0:T(2,128)} %constant.12.clone.spots_hbm, s32[512]{0:T(512)} %source_hbm.1, s32[512]{0:T(512)} %target_hbm.1, bf16[512,128,128]{2,1,0:T(8,128)(2,1)} %adjacency_hbm.1), custom_call_target="tpu_custom_call" | custom-call | flops 8388608 | bytes 16777216 | tf_op jit(solution)/shard_map/load/pallas_call | solution.py:247
  11.4 0.0 collective-permute-done.across_ref
  11.4 0.3 mix.2
  11.7 1.4 %collective-permute-start.1 = (bf16[512,256]{1,0:T(8,128)(2,1)S(1)}, bf16[512,256]{1,0:T(8,128)(2,1)S(1)}, u32[]{:S(2)}, u32[]{:S(2)}) collective-permute-start(bf16[512,256]{1,0:T(8,128)(2,1)S(1)} %mix.2), channel_id=1, source_target_pairs={{0,4},{1,5},{2,34},{3,35},{4,8},{5,9},{6,38},{7,39},{8,12},{9,13},... | collective-permute-start | bytes 786440 | tf_op jit(solution)/shard_map/ppermute | solution.py:57
  13.0 1.5 %collective-permute-start.2 = (bf16[512,256]{1,0:T(8,128)(2,1)S(1)}, bf16[512,256]{1,0:T(8,128)(2,1)S(1)}, u32[]{:S(2)}, u32[]{:S(2)}) collective-permute-start(bf16[512,256]{1,0:T(8,128)(2,1)S(1)} %mix.2), channel_id=1, source_target_pairs={{0,12},{1,13},{2,98},{3,99},{4,0},{5,1},{6,102},{7,103},{8,4},{9,5... | collective-permute-start | bytes 786440 | tf_op jit(solution)/shard_map/ppermute | solution.py:57
  14.6 1.6 %collective-permute-start.6 = (bf16[512,256]{1,0:T(8,128)(2,1)S(1)}, bf16[512,256]{1,0:T(8,128)(2,1)S(1)}, u32[]{:S(2)}, u32[]{:S(2)}) collective-permute-start(bf16[512,256]{1,0:T(8,128)(2,1)S(1)} %mix.2), channel_id=1, source_target_pairs={{0,8},{1,9},{2,66},{3,67},{4,12},{5,13},{6,70},{7,71},{8,0},{9,1},... | collective-permute-start | bytes 786440 | tf_op jit(solution)/shard_map/ppermute | solution.py:57
  16.1 3.4 %collective-permute-start.4 = (bf16[512,256]{1,0:T(8,128)(2,1)S(1)}, bf16[512,256]{1,0:T(8,128)(2,1)S(1)}, u32[]{:S(2)}, u32[]{:S(2)}) collective-permute-start(bf16[512,256]{1,0:T(8,128)(2,1)S(1)} %mix.2), channel_id=1, source_target_pairs={{0,16},{1,17},{2,18},{3,19},{4,20},{5,21},{6,22},{7,23},{8,24},{9,... | collective-permute-start | bytes 786440 | tf_op jit(solution)/shard_map/ppermute | solution.py:57
  19.5 0.0 collective-permute-done.1
  19.6 0.0 copy-start
  19.6 1.1 %collective-permute-done.2 = bf16[512,256]{1,0:T(8,128)(2,1)S(1)} collective-permute-done((bf16[512,256]{1,0:T(8,128)(2,1)S(1)}, bf16[512,256]{1,0:T(8,128)(2,1)S(1)}, u32[]{:S(2)}, u32[]{:S(2)}) %collective-permute-start.2) | collective-permute-done | bytes 262176 | tf_op jit(solution)/shard_map/ppermute | solution.py:57
  20.7 1.8 %collective-permute-done.6 = bf16[512,256]{1,0:T(8,128)(2,1)S(1)} collective-permute-done((bf16[512,256]{1,0:T(8,128)(2,1)S(1)}, bf16[512,256]{1,0:T(8,128)(2,1)S(1)}, u32[]{:S(2)}, u32[]{:S(2)}) %collective-permute-start.6) | collective-permute-done | bytes 262176 | tf_op jit(solution)/shard_map/ppermute | solution.py:57
  22.5 2.0 %collective-permute-done.4 = bf16[512,256]{1,0:T(8,128)(2,1)S(1)} collective-permute-done((bf16[512,256]{1,0:T(8,128)(2,1)S(1)}, bf16[512,256]{1,0:T(8,128)(2,1)S(1)}, u32[]{:S(2)}, u32[]{:S(2)}) %collective-permute-start.4) | collective-permute-done | bytes 262176 | tf_op jit(solution)/shard_map/ppermute | solution.py:57
  24.5 4.2 %collective-permute-start.10 = (bf16[2560,256]{1,0:T(8,128)(2,1)S(1)}, bf16[2560,256]{1,0:T(8,128)(2,1)S(1)}, u32[]{:S(2)}, u32[]{:S(2)}) collective-permute-start(bf16[2560,256]{1,0:T(8,128)(2,1)S(1)} %constant_dynamic-update-slice_fusion.refs_0_), channel_id=1, source_target_pairs={{0,96},{1,97},{2,14},{3,15},{4,100},{5,101},{6,2},{7,3},{8,104},{9... | collective-permute-start | bytes 3932168 | tf_op jit(solution)/shard_map/ppermute | solution.py:57
  28.8 0.0 collective-permute-start.7
  28.8 2.8 %collective-permute-start.3 = (bf16[1024,256]{1,0:T(8,128)(2,1)S(1)}, bf16[1024,256]{1,0:T(8,128)(2,1)S(1)}, u32[]{:S(2)}, u32[]{:S(2)}) collective-permute-start(bf16[1024,256]{1,0:T(8,128)(2,1)S(1)} %pad_maximum_fusion.2), channel_id=1, source_target_pairs={{0,16},{1,17},{2,18},{3,19},{4,20},{5,21},{6,22},{7,23},{8,24},{9,... | collective-permute-start | bytes 1572872 | tf_op jit(solution)/shard_map/ppermute | solution.py:57
  31.7 0.9 %collective-permute-start.13 = (bf16[2560,256]{1,0:T(8,128)(2,1)S(1)}, bf16[2560,256]{1,0:T(8,128)(2,1)S(1)}, u32[]{:S(2)}, u32[]{:S(2)}) collective-permute-start(bf16[2560,256]{1,0:T(8,128)(2,1)S(1)} %constant_dynamic-update-slice_fusion.refs_0_), channel_id=1, source_target_pairs={{0,2},{1,3},{2,0},{3,1},{4,6},{5,7},{6,4},{7,5},{8,10},{9,11},{10,... | collective-permute-start | bytes 3932168 | tf_op jit(solution)/shard_map/ppermute | solution.py:57
  32.5 1.9 %collective-permute-start.5 = (bf16[512,256]{1,0:T(8,128)(2,1)S(1)}, bf16[512,256]{1,0:T(8,128)(2,1)S(1)}, u32[]{:S(2)}, u32[]{:S(2)}) collective-permute-start(bf16[512,256]{1,0:T(8,128)(2,1)S(1)} %collective-permute-done.4), channel_id=1, source_target_pairs={{0,8},{1,9},{2,66},{3,67},{4,12},{5,13},{6,70},{7,71},{8,0},{9,1},... | collective-permute-start | bytes 786440 | tf_op jit(solution)/shard_map/ppermute | solution.py:57
  34.5 0.0 copy-done
  34.5 0.3 mix.3.refs_4_
  34.8 9.0 %collective-permute-done.3 = bf16[1024,256]{1,0:T(8,128)(2,1)S(1)} collective-permute-done((bf16[1024,256]{1,0:T(8,128)(2,1)S(1)}, bf16[1024,256]{1,0:T(8,128)(2,1)S(1)}, u32[]{:S(2)}, u32[]{:S(2)}) %collective-permute-start.3) | collective-permute-done | bytes 524320 | tf_op jit(solution)/shard_map/ppermute | solution.py:57
  43.8 0.0 collective-permute-done.5
  43.9 1.0 %collective-permute-start.9 = (bf16[1536,256]{1,0:T(8,128)(2,1)S(1)}, bf16[1536,256]{1,0:T(8,128)(2,1)S(1)}, u32[]{:S(2)}, u32[]{:S(2)}) collective-permute-start(bf16[1536,256]{1,0:T(8,128)(2,1)S(1)} %constant_dynamic-update-slice_fusion.5.refs_0_), channel_id=1, source_target_pairs={{0,2},{1,3},{2,0},{3,1},{4,6},{5,7},{6,4},{7,5},{8,10},{9,11},{10,... | collective-permute-start | bytes 2359304 | tf_op jit(solution)/shard_map/ppermute | solution.py:57
  44.9 1.2 %collective-permute-done.10.refs_1_ = bf16[2560,256]{1,0:T(8,128)(2,1)S(1)} collective-permute-done((bf16[2560,256]{1,0:T(8,128)(2,1)S(1)}, bf16[2560,256]{1,0:T(8,128)(2,1)S(1)}, u32[]{:S(2)}, u32[]{:S(2)}) %collective-permute-start.10) | collective-permute-done | bytes 1310752 | tf_op jit(solution)/shard_map/ppermute | solution.py:57
  46.2 0.1 pad_maximum_fusion.1
  46.3 3.5 %collective-permute-start.15 = (bf16[2560,256]{1,0:T(8,128)(2,1)S(1)}, bf16[2560,256]{1,0:T(8,128)(2,1)S(1)}, u32[]{:S(2)}, u32[]{:S(2)}) collective-permute-start(bf16[2560,256]{1,0:T(8,128)(2,1)S(1)} %pad_maximum_fusion.1), channel_id=1, source_target_pairs={{0,96},{1,97},{2,14},{3,15},{4,100},{5,101},{6,2},{7,3},{8,104},{9... | collective-permute-start | bytes 3932168 | tf_op jit(solution)/shard_map/ppermute | solution.py:57
  49.7 0.0 collective-permute-done.7.refs_0_
  49.7 0.1 slice.16
  49.8 0.1 pad_maximum_fusion
  49.9 0.1 collective-permute-start.8
  50.0 1.1 %collective-permute-start.11 = (bf16[2560,256]{1,0:T(8,128)(2,1)S(1)}, bf16[2560,256]{1,0:T(8,128)(2,1)S(1)}, u32[]{:S(2)}, u32[]{:S(2)}) collective-permute-start(bf16[2560,256]{1,0:T(8,128)(2,1)S(1)} %collective-permute-done.7.refs_0_), channel_id=1, source_target_pairs={{0,2},{1,3},{2,0},{3,1},{4,6},{5,7},{6,4},{7,5},{8,10},{9,11},{10,... | collective-permute-start | bytes 3932168 | tf_op jit(solution)/shard_map/ppermute | solution.py:57
  51.1 0.0 collective-permute-done.13.refs_1_
  51.1 0.1 collective-permute-start.12
  51.2 2.1 %gather.6.refs_4_ = f32[512,256]{1,0:T(8,128)S(1)} custom-call(s32[1024]{0:T(1024)S(1)} %get-tuple-element.14.table_ref, bf16[513,128,128]{2,1,0:T(8,128)(2,1)S(1)} %get-tuple-element.15.tiles_ref, bf16[2560,256]{1,0:T(8,128)(2,1)S(1)} %constant_dynamic-update-slice_fusion.refs_0_, bf16[2560,256]{1,0:T(8,128)(2,1)S(1)} %collective-permute-done.13.refs_1_), custom_call_target="tpu_custom_call" | custom-call | flops 26843545600 | bytes 3932160 | tf_op jit(solution)/shard_map/gather/pallas_call | solution.py:326
  53.3 0.4 collective-permute-done.11.refs_2_
  53.7 1.9 %collective-permute-done.12.refs_3_ = bf16[2560,256]{1,0:T(8,128)(2,1)S(1)} collective-permute-done((bf16[2560,256]{1,0:T(8,128)(2,1)S(1)}, bf16[2560,256]{1,0:T(8,128)(2,1)S(1)}, u32[]{:S(2)}, u32[]{:S(2)}) %collective-permute-start.12) | collective-permute-done | bytes 1310752 | tf_op jit(solution)/shard_map/ppermute | solution.py:57
  55.6 3.5 %gather.7.refs_2_ = f32[512,256]{1,0:T(8,128)S(1)} custom-call(s32[1024]{0:T(1024)S(1)} %get-tuple-element.14.table_ref, bf16[513,128,128]{2,1,0:T(8,128)(2,1)S(1)} %get-tuple-element.15.tiles_ref, bf16[2560,256]{1,0:T(8,128)(2,1)S(1)} %collective-permute-done.7.refs_0_, bf16[2560,256]{1,0:T(8,128)(2,1)S(1)} %collective-permute-done.10.refs_1_, ...), custom_call_target="tpu_custom_call" | custom-call | flops 53687091200 | bytes 7864320 | tf_op jit(solution)/shard_map/gather/pallas_call | solution.py:326
  59.1 5.2 %collective-permute-done.15.refs_1_ = bf16[2560,256]{1,0:T(8,128)(2,1)S(1)} collective-permute-done((bf16[2560,256]{1,0:T(8,128)(2,1)S(1)}, bf16[2560,256]{1,0:T(8,128)(2,1)S(1)}, u32[]{:S(2)}, u32[]{:S(2)}) %collective-permute-start.15) | collective-permute-done | bytes 1310752 | tf_op jit(solution)/shard_map/ppermute | solution.py:57
  64.3 0.0 collective-permute-done.9.refs_1_
  64.3 1.6 %gather.8.refs_2_ = f32[512,256]{1,0:T(8,128)S(1)} custom-call(s32[1024]{0:T(1024)S(1)} %get-tuple-element.14.table_ref, bf16[513,128,128]{2,1,0:T(8,128)(2,1)S(1)} %get-tuple-element.15.tiles_ref, bf16[1536,256]{1,0:T(8,128)(2,1)S(1)} %constant_dynamic-update-slice_fusion.5.refs_0_, bf16[1536,256]{1,0:T(8,128)(2,1)S(1)} %collective-permute-done.9.refs_1_, ...), custom_call_target="tpu_custom_call" | custom-call | flops 16106127360 | bytes 2359296 | tf_op jit(solution)/shard_map/gather/pallas_call | solution.py:326
  65.9 3.5 %collective-permute-start.16 = (bf16[1024,256]{1,0:T(8,128)(2,1)S(1)}, bf16[1024,256]{1,0:T(8,128)(2,1)S(1)}, u32[]{:S(2)}, u32[]{:S(2)}) collective-permute-start(bf16[1024,256]{1,0:T(8,128)(2,1)S(1)} %slice.19), channel_id=1, source_target_pairs={{0,96},{1,97},{2,14},{3,15},{4,100},{5,101},{6,2},{7,3},{8,104},{9... | collective-permute-start | bytes 1572872 | tf_op jit(solution)/shard_map/ppermute | solution.py:57
  69.4 1.8 %collective-permute-start.19 = (bf16[2560,256]{1,0:T(8,128)(2,1)S(1)}, bf16[2560,256]{1,0:T(8,128)(2,1)S(1)}, u32[]{:S(2)}, u32[]{:S(2)}) collective-permute-start(bf16[2560,256]{1,0:T(8,128)(2,1)S(1)} %collective-permute-done.15.refs_1_), channel_id=1, source_target_pairs={{0,2},{1,3},{2,0},{3,1},{4,6},{5,7},{6,4},{7,5},{8,10},{9,11},{10,... | collective-permute-start | bytes 3932168 | tf_op jit(solution)/shard_map/ppermute | solution.py:57
  71.2 0.0 collective-permute-done.8.refs_0_
  71.3 0.4 collective-permute-start.14
  71.6 1.3 %collective-permute-start.18 = (bf16[3072,256]{1,0:T(8,128)(2,1)S(1)}, bf16[3072,256]{1,0:T(8,128)(2,1)S(1)}, u32[]{:S(2)}, u32[]{:S(2)}) collective-permute-start(bf16[3072,256]{1,0:T(8,128)(2,1)S(1)} %collective-permute-done.8.refs_0_), channel_id=1, source_target_pairs={{0,2},{1,3},{2,0},{3,1},{4,6},{5,7},{6,4},{7,5},{8,10},{9,11},{10,... | collective-permute-start | bytes 4718600 | tf_op jit(solution)/shard_map/ppermute | solution.py:57
  72.9 2.2 %gather.9.refs_2_ = f32[512,256]{1,0:T(8,128)S(1)} custom-call(s32[1024]{0:T(1024)S(1)} %get-tuple-element.14.table_ref, bf16[513,128,128]{2,1,0:T(8,128)(2,1)S(1)} %get-tuple-element.15.tiles_ref, bf16[3072,256]{1,0:T(8,128)(2,1)S(1)} %collective-permute-done.8.refs_0_, bf16[2560,256]{1,0:T(8,128)(2,1)S(1)} %collective-permute-done.15.refs_1_, ...), custom_call_target="tpu_custom_call" | custom-call | flops 29527900160 | bytes 4325376 | tf_op jit(solution)/shard_map/gather/pallas_call | solution.py:326
  75.2 2.9 %collective-permute-done.14 = bf16[512,256]{1,0:T(8,128)(2,1)S(1)} collective-permute-done((bf16[512,256]{1,0:T(8,128)(2,1)S(1)}, bf16[512,256]{1,0:T(8,128)(2,1)S(1)}, u32[]{:S(2)}, u32[]{:S(2)}) %collective-permute-start.14) | collective-permute-done | bytes 262176 | tf_op jit(solution)/shard_map/ppermute | solution.py:57
  78.1 0.0 collective-permute-done.16
  78.1 2.3 %collective-permute-start.17 = (bf16[1536,256]{1,0:T(8,128)(2,1)S(1)}, bf16[1536,256]{1,0:T(8,128)(2,1)S(1)}, u32[]{:S(2)}, u32[]{:S(2)}) collective-permute-start(bf16[1536,256]{1,0:T(8,128)(2,1)S(1)} %constant_dynamic-update-slice_fusion.7.refs_0_), channel_id=1, source_target_pairs={{0,2},{1,3},{2,0},{3,1},{4,6},{5,7},{6,4},{7,5},{8,10},{9,11},{10,... | collective-permute-start | bytes 2359304 | tf_op jit(solution)/shard_map/ppermute | solution.py:57
  80.4 0.0 collective-permute-done.19.refs_1_
  80.4 0.0 collective-permute-done.18.refs_0_
  80.4 2.2 %gather.10.refs_2_ = f32[512,256]{1,0:T(8,128)S(1)} custom-call(s32[1024]{0:T(1024)S(1)} %get-tuple-element.14.table_ref, bf16[513,128,128]{2,1,0:T(8,128)(2,1)S(1)} %get-tuple-element.15.tiles_ref, bf16[3072,256]{1,0:T(8,128)(2,1)S(1)} %collective-permute-done.18.refs_0_, bf16[2560,256]{1,0:T(8,128)(2,1)S(1)} %collective-permute-done.19.refs_1_, ...), custom_call_target="tpu_custom_call" | custom-call | flops 29527900160 | bytes 4325376 | tf_op jit(solution)/shard_map/gather/pallas_call | solution.py:326
  82.7 0.0 collective-permute-done.17.refs_1_
  82.7 2.3 %gather.11 = bf16[512,256]{1,0:T(8,128)(2,1)} custom-call(s32[1024]{0:T(1024)S(1)} %get-tuple-element.14.table_ref, bf16[513,128,128]{2,1,0:T(8,128)(2,1)S(1)} %get-tuple-element.15.tiles_ref, bf16[1536,256]{1,0:T(8,128)(2,1)S(1)} %constant_dynamic-update-slice_fusion.7.refs_0_, bf16[1536,256]{1,0:T(8,128)(2,1)S(1)} %collective-permute-done.17.refs_1_, ...), custom_call_target="tpu_custom_call" | custom-call | flops 16106127360 | bytes 2359296 | tf_op jit(solution)/shard_map/gather/pallas_call | solution.py:326
  (13 shorter events, 0.3 us)
Async XLA Ops:
  1.2 10.1 %collective-permute-start = (bf16[512,256]{1,0:T(8,128)(2,1)S(1)}, bf16[512,256]{1,0:T(8,128)(2,1)S(1)}, u32[]{:S(2)}, u32[]{:S(2)}) collective-permute-start(bf16[512,256]{1,0:T(8,128)(2,1)S(1)} %get-tuple-element.16.features_ref), channel_id=1, source_target_pairs={{0,1},{1,0},{2,3},{3,2},{4,5},{5,4},{6,7},{7,6},{8,9},{9,8},{10,11... | collective-permute-start | bytes 786440 | tf_op jit(solution)/shard_map/ppermute | solution.py:57
  11.7 7.9 %collective-permute-start.1 = (bf16[512,256]{1,0:T(8,128)(2,1)S(1)}, bf16[512,256]{1,0:T(8,128)(2,1)S(1)}, u32[]{:S(2)}, u32[]{:S(2)}) collective-permute-start(bf16[512,256]{1,0:T(8,128)(2,1)S(1)} %mix.2), channel_id=1, source_target_pairs={{0,4},{1,5},{2,34},{3,35},{4,8},{5,9},{6,38},{7,39},{8,12},{9,13},... | collective-permute-start | bytes 786440 | tf_op jit(solution)/shard_map/ppermute | solution.py:57
  13.0 7.6 %collective-permute-start.2 = (bf16[512,256]{1,0:T(8,128)(2,1)S(1)}, bf16[512,256]{1,0:T(8,128)(2,1)S(1)}, u32[]{:S(2)}, u32[]{:S(2)}) collective-permute-start(bf16[512,256]{1,0:T(8,128)(2,1)S(1)} %mix.2), channel_id=1, source_target_pairs={{0,12},{1,13},{2,98},{3,99},{4,0},{5,1},{6,102},{7,103},{8,4},{9,5... | collective-permute-start | bytes 786440 | tf_op jit(solution)/shard_map/ppermute | solution.py:57
  14.6 8.0 %collective-permute-start.6 = (bf16[512,256]{1,0:T(8,128)(2,1)S(1)}, bf16[512,256]{1,0:T(8,128)(2,1)S(1)}, u32[]{:S(2)}, u32[]{:S(2)}) collective-permute-start(bf16[512,256]{1,0:T(8,128)(2,1)S(1)} %mix.2), channel_id=1, source_target_pairs={{0,8},{1,9},{2,66},{3,67},{4,12},{5,13},{6,70},{7,71},{8,0},{9,1},... | collective-permute-start | bytes 786440 | tf_op jit(solution)/shard_map/ppermute | solution.py:57
  16.1 8.4 %collective-permute-start.4 = (bf16[512,256]{1,0:T(8,128)(2,1)S(1)}, bf16[512,256]{1,0:T(8,128)(2,1)S(1)}, u32[]{:S(2)}, u32[]{:S(2)}) collective-permute-start(bf16[512,256]{1,0:T(8,128)(2,1)S(1)} %mix.2), channel_id=1, source_target_pairs={{0,16},{1,17},{2,18},{3,19},{4,20},{5,21},{6,22},{7,23},{8,24},{9,... | collective-permute-start | bytes 786440 | tf_op jit(solution)/shard_map/ppermute | solution.py:57
  19.6 14.9 %copy-start = (f32[256]{0:T(256)S(1)}, f32[256]{0:T(256)}, u32[]{:S(2)}) copy-start(f32[256]{0:T(256)} %param.14) | copy-start | bytes 3076
  24.5 21.6 %collective-permute-start.10 = (bf16[2560,256]{1,0:T(8,128)(2,1)S(1)}, bf16[2560,256]{1,0:T(8,128)(2,1)S(1)}, u32[]{:S(2)}, u32[]{:S(2)}) collective-permute-start(bf16[2560,256]{1,0:T(8,128)(2,1)S(1)} %constant_dynamic-update-slice_fusion.refs_0_), channel_id=1, source_target_pairs={{0,96},{1,97},{2,14},{3,15},{4,100},{5,101},{6,2},{7,3},{8,104},{9... | collective-permute-start | bytes 3932168 | tf_op jit(solution)/shard_map/ppermute | solution.py:57
  28.8 21.0 %collective-permute-start.7 = (bf16[2560,256]{1,0:T(8,128)(2,1)S(1)}, bf16[2560,256]{1,0:T(8,128)(2,1)S(1)}, u32[]{:S(2)}, u32[]{:S(2)}) collective-permute-start(bf16[2560,256]{1,0:T(8,128)(2,1)S(1)} %constant_dynamic-update-slice_fusion.refs_0_), channel_id=1, source_target_pairs={{0,32},{1,33},{2,6},{3,7},{4,36},{5,37},{6,10},{7,11},{8,40},{9,41... | collective-permute-start | bytes 3932168 | tf_op jit(solution)/shard_map/ppermute | solution.py:57
  28.8 15.0 %collective-permute-start.3 = (bf16[1024,256]{1,0:T(8,128)(2,1)S(1)}, bf16[1024,256]{1,0:T(8,128)(2,1)S(1)}, u32[]{:S(2)}, u32[]{:S(2)}) collective-permute-start(bf16[1024,256]{1,0:T(8,128)(2,1)S(1)} %pad_maximum_fusion.2), channel_id=1, source_target_pairs={{0,16},{1,17},{2,18},{3,19},{4,20},{5,21},{6,22},{7,23},{8,24},{9,... | collective-permute-start | bytes 1572872 | tf_op jit(solution)/shard_map/ppermute | solution.py:57
  31.7 19.4 %collective-permute-start.13 = (bf16[2560,256]{1,0:T(8,128)(2,1)S(1)}, bf16[2560,256]{1,0:T(8,128)(2,1)S(1)}, u32[]{:S(2)}, u32[]{:S(2)}) collective-permute-start(bf16[2560,256]{1,0:T(8,128)(2,1)S(1)} %constant_dynamic-update-slice_fusion.refs_0_), channel_id=1, source_target_pairs={{0,2},{1,3},{2,0},{3,1},{4,6},{5,7},{6,4},{7,5},{8,10},{9,11},{10,... | collective-permute-start | bytes 3932168 | tf_op jit(solution)/shard_map/ppermute | solution.py:57
  32.5 11.3 %collective-permute-start.5 = (bf16[512,256]{1,0:T(8,128)(2,1)S(1)}, bf16[512,256]{1,0:T(8,128)(2,1)S(1)}, u32[]{:S(2)}, u32[]{:S(2)}) collective-permute-start(bf16[512,256]{1,0:T(8,128)(2,1)S(1)} %collective-permute-done.4), channel_id=1, source_target_pairs={{0,8},{1,9},{2,66},{3,67},{4,12},{5,13},{6,70},{7,71},{8,0},{9,1},... | collective-permute-start | bytes 786440 | tf_op jit(solution)/shard_map/ppermute | solution.py:57
  43.9 20.5 %collective-permute-start.9 = (bf16[1536,256]{1,0:T(8,128)(2,1)S(1)}, bf16[1536,256]{1,0:T(8,128)(2,1)S(1)}, u32[]{:S(2)}, u32[]{:S(2)}) collective-permute-start(bf16[1536,256]{1,0:T(8,128)(2,1)S(1)} %constant_dynamic-update-slice_fusion.5.refs_0_), channel_id=1, source_target_pairs={{0,2},{1,3},{2,0},{3,1},{4,6},{5,7},{6,4},{7,5},{8,10},{9,11},{10,... | collective-permute-start | bytes 2359304 | tf_op jit(solution)/shard_map/ppermute | solution.py:57
  46.3 18.0 %collective-permute-start.15 = (bf16[2560,256]{1,0:T(8,128)(2,1)S(1)}, bf16[2560,256]{1,0:T(8,128)(2,1)S(1)}, u32[]{:S(2)}, u32[]{:S(2)}) collective-permute-start(bf16[2560,256]{1,0:T(8,128)(2,1)S(1)} %pad_maximum_fusion.1), channel_id=1, source_target_pairs={{0,96},{1,97},{2,14},{3,15},{4,100},{5,101},{6,2},{7,3},{8,104},{9... | collective-permute-start | bytes 3932168 | tf_op jit(solution)/shard_map/ppermute | solution.py:57
  49.9 21.3 %collective-permute-start.8 = (bf16[3072,256]{1,0:T(8,128)(2,1)S(1)}, bf16[3072,256]{1,0:T(8,128)(2,1)S(1)}, u32[]{:S(2)}, u32[]{:S(2)}) collective-permute-start(bf16[3072,256]{1,0:T(8,128)(2,1)S(1)} %pad_maximum_fusion), channel_id=1, source_target_pairs={{0,32},{1,33},{2,6},{3,7},{4,36},{5,37},{6,10},{7,11},{8,40},{9,41... | collective-permute-start | bytes 4718600 | tf_op jit(solution)/shard_map/ppermute | solution.py:57
  50.0 3.7 %collective-permute-start.11 = (bf16[2560,256]{1,0:T(8,128)(2,1)S(1)}, bf16[2560,256]{1,0:T(8,128)(2,1)S(1)}, u32[]{:S(2)}, u32[]{:S(2)}) collective-permute-start(bf16[2560,256]{1,0:T(8,128)(2,1)S(1)} %collective-permute-done.7.refs_0_), channel_id=1, source_target_pairs={{0,2},{1,3},{2,0},{3,1},{4,6},{5,7},{6,4},{7,5},{8,10},{9,11},{10,... | collective-permute-start | bytes 3932168 | tf_op jit(solution)/shard_map/ppermute | solution.py:57
  51.1 4.5 %collective-permute-start.12 = (bf16[2560,256]{1,0:T(8,128)(2,1)S(1)}, bf16[2560,256]{1,0:T(8,128)(2,1)S(1)}, u32[]{:S(2)}, u32[]{:S(2)}) collective-permute-start(bf16[2560,256]{1,0:T(8,128)(2,1)S(1)} %collective-permute-done.10.refs_1_), channel_id=1, source_target_pairs={{0,2},{1,3},{2,0},{3,1},{4,6},{5,7},{6,4},{7,5},{8,10},{9,11},{10,... | collective-permute-start | bytes 3932168 | tf_op jit(solution)/shard_map/ppermute | solution.py:57
  65.9 12.2 %collective-permute-start.16 = (bf16[1024,256]{1,0:T(8,128)(2,1)S(1)}, bf16[1024,256]{1,0:T(8,128)(2,1)S(1)}, u32[]{:S(2)}, u32[]{:S(2)}) collective-permute-start(bf16[1024,256]{1,0:T(8,128)(2,1)S(1)} %slice.19), channel_id=1, source_target_pairs={{0,96},{1,97},{2,14},{3,15},{4,100},{5,101},{6,2},{7,3},{8,104},{9... | collective-permute-start | bytes 1572872 | tf_op jit(solution)/shard_map/ppermute | solution.py:57
  69.4 11.0 %collective-permute-start.19 = (bf16[2560,256]{1,0:T(8,128)(2,1)S(1)}, bf16[2560,256]{1,0:T(8,128)(2,1)S(1)}, u32[]{:S(2)}, u32[]{:S(2)}) collective-permute-start(bf16[2560,256]{1,0:T(8,128)(2,1)S(1)} %collective-permute-done.15.refs_1_), channel_id=1, source_target_pairs={{0,2},{1,3},{2,0},{3,1},{4,6},{5,7},{6,4},{7,5},{8,10},{9,11},{10,... | collective-permute-start | bytes 3932168 | tf_op jit(solution)/shard_map/ppermute | solution.py:57
  71.3 6.8 %collective-permute-start.14 = (bf16[512,256]{1,0:T(8,128)(2,1)S(1)}, bf16[512,256]{1,0:T(8,128)(2,1)S(1)}, u32[]{:S(2)}, u32[]{:S(2)}) collective-permute-start(bf16[512,256]{1,0:T(8,128)(2,1)S(1)} %slice.17), channel_id=1, source_target_pairs={{0,32},{1,33},{2,6},{3,7},{4,36},{5,37},{6,10},{7,11},{8,40},{9,41... | collective-permute-start | bytes 786440 | tf_op jit(solution)/shard_map/ppermute | solution.py:57
  71.6 8.8 %collective-permute-start.18 = (bf16[3072,256]{1,0:T(8,128)(2,1)S(1)}, bf16[3072,256]{1,0:T(8,128)(2,1)S(1)}, u32[]{:S(2)}, u32[]{:S(2)}) collective-permute-start(bf16[3072,256]{1,0:T(8,128)(2,1)S(1)} %collective-permute-done.8.refs_0_), channel_id=1, source_target_pairs={{0,2},{1,3},{2,0},{3,1},{4,6},{5,7},{6,4},{7,5},{8,10},{9,11},{10,... | collective-permute-start | bytes 4718600 | tf_op jit(solution)/shard_map/ppermute | solution.py:57
  78.1 4.5 %collective-permute-start.17 = (bf16[1536,256]{1,0:T(8,128)(2,1)S(1)}, bf16[1536,256]{1,0:T(8,128)(2,1)S(1)}, u32[]{:S(2)}, u32[]{:S(2)}) collective-permute-start(bf16[1536,256]{1,0:T(8,128)(2,1)S(1)} %constant_dynamic-update-slice_fusion.7.refs_0_), channel_id=1, source_target_pairs={{0,2},{1,3},{2,0},{3,1},{4,6},{5,7},{6,4},{7,5},{8,10},{9,11},{10,... | collective-permute-start | bytes 2359304 | tf_op jit(solution)/shard_map/ppermute | solution.py:57
